TPU v7x, 32 devices: a whole 2x2x4 slice. The times are simulated.
32 devices in a mesh: depth: 4 (over z), phi: 8 (over y, x, core).
Axes of the slice: x: 2, y: 2, z: 4, core: 2. Of those that a mesh axis runs over, the one named last changes fastest.
Arguments:
- grad_out: bfloat16 [448, 32, 32, 128], P('depth', 'phi'), may hold values from -6 to 6
- pre_act: bfloat16 [448, 32, 32, 128], P('depth', 'phi'), may hold values from -8 to 8
- w_first: bfloat16 [3, 3, 3, 32, 32], replicated, may hold values from -0.21875 to 0.21875
- w_second: bfloat16 [3, 3, 3, 32, 32], replicated, may hold values from -0.21875 to 0.21875
- map_blocks: bfloat16 [4096, 128, 128], P(('depth', 'phi')), may hold values from -0.15625 to 0.15625
- row_block: int32 [4096], P(('depth', 'phi')), may hold values from 0 to 447
- owner: int32 [4096, 1], P(('depth', 'phi')), may hold values from 0 to 31; in each aligned block of 128 rows (0 to 127, 128 to 255, ...) at most 8 rows name the same one
- col_local: int32 [4096], P(('depth', 'phi')), may hold values from 0 to 11
Outputs:
- cell_grad: float32 [384, 32, 128], P(('depth', 'phi'))
Inputs may be any that keep to these rules, and one draw needn't show every extreme that they name: Among the 128 blocks of one device no owner is named more than 8 times, and in some devices one owner is named exactly 8 times; every owner is named by some block.
All inputs are finite; a program needn't handle non-finite values.
Results may differ from a plain program's by a relative error of at most 0.0033.
Values may be sent and summed in bfloat16 or wider, within the bound.
A program may use at most 192 MiB of HBM per device.

v0:
```python
import jax
import jax.numpy as jnp
from jax import lax
from jax.experimental import pallas as pl
from jax.experimental.pallas import tpu as pltpu
from jax.sharding import PartitionSpec as P

CB_DEV = 12
VMEM_LIMIT = 48 * 1024 * 1024


def shift(block, axis, step, periodic):
    count = lax.axis_size(axis)
    pairs = [(i, i + step) for i in range(count) if 0 <= i + step < count]
    if periodic:
        pairs = [(i, (i + step) % count) for i in range(count)]
    return lax.ppermute(block, axis, pairs)


def edges_of(first_layer, last_layer):
    below = shift(last_layer, "depth", 1, False)
    above = shift(first_layer, "depth", -1, False)
    layers = jnp.stack([below, above])
    corner_low = shift(layers[:, -1], "phi", 1, True)
    corner_high = shift(layers[:, 0], "phi", -1, True)
    middle = layers.reshape(2, -1, layers.shape[-1])
    return jnp.concatenate([corner_low, middle, corner_high], axis=1)


def mixing(weight, phi_len):
    channels = weight.shape[3]
    base = jnp.transpose(weight[::-1, ::-1], (2, 3, 0, 1, 4))
    base = base.reshape(3, channels, 3, 3 * channels)
    rows = [
        jnp.pad(base, ((0, 0), (0, 0), (0, 0), (p * channels, (phi_len - 1 - p) * channels)))
        for p in range(phi_len)
    ]
    full = jnp.stack(rows, axis=1)
    return full.reshape(3 * phi_len * channels, 3 * (phi_len + 2) * channels)


def fill(xp, x_ref, low_ref, high_ref, edge_ref):
    depth = low_ref.shape[0]
    xp[0] = edge_ref[0]
    xp[depth + 1] = edge_ref[1]

    def step(z, carry):
        for k in range(4):
            d = z * 4 + k
            xp[d + 1, 0:32] = low_ref[d]
            xp[d + 1, 32:160] = x_ref[pl.ds(d * 4, 4)].reshape(128, 128)
            xp[d + 1, 160:192] = high_ref[d]
        return carry

    lax.fori_loop(0, depth // 4, step, 0)


def conv_pair(xp, w_ref, z):
    slabs = [xp[z + k] for k in range(4)]
    rhs = jnp.concatenate(
        [jnp.concatenate([slabs[k], slabs[k + 1]], axis=1) for k in range(3)], axis=0
    )
    y = jnp.dot(w_ref[...], rhs, preferred_element_type=jnp.float32)
    lane = lax.broadcasted_iota(jnp.int32, (128, 128), 1)
    outs = []
    for k in range(2):
        cols = slice(128 * k, 128 * k + 128)
        minus = pltpu.roll(y[0:128, cols], 127, 1)
        plus = pltpu.roll(y[256:384, cols], 1, 1)
        outs.append(
            y[128:256, cols]
            + jnp.where(lane == 127, 0.0, minus)
            + jnp.where(lane == 0, 0.0, plus)
        )
    return outs


def first_kernel(x_ref, low_ref, high_ref, edge_ref, pre_ref, w_ref, hid_ref, f0_ref, f3_ref, xp):
    fill(xp, x_ref, low_ref, high_ref, edge_ref)
    depth = low_ref.shape[0]

    def step(t, carry):
        z = t * 2
        for k, back in enumerate(conv_pair(xp, w_ref, z)):
            p = pre_ref[pl.ds((z + k) * 4, 4)].reshape(128, 128).astype(jnp.float32)
            s = 1.0 / (1.0 + jnp.exp(-p))
            hid = (back * s * (1.0 + p * (1.0 - s))).astype(jnp.bfloat16)
            hid_ref[pl.ds((z + k) * 4, 4)] = hid.reshape(4, 32, 128)
            f0_ref[z + k] = hid[0:32]
            f3_ref[z + k] = hid[96:128]
        return carry

    lax.fori_loop(0, depth // 2, step, 0)


def second_kernel(
    row_ref, pos_ref, x_ref, low_ref, high_ref, edge_ref, grad_ref, w_ref, map_ref, buf_ref, xp, grid
):
    fill(xp, x_ref, low_ref, high_ref, edge_ref)
    depth = low_ref.shape[0]

    def step(t, carry):
        z = t * 2
        for k, back in enumerate(conv_pair(xp, w_ref, z)):
            g = grad_ref[pl.ds((z + k) * 4, 4)].reshape(128, 128).astype(jnp.float32)
            grid[pl.ds((z + k) * 4, 4)] = (back + g).astype(jnp.bfloat16).reshape(4, 32, 128)
        return carry

    lax.fori_loop(0, depth // 2, step, 0)

    def clear(t, carry):
        buf_ref[pl.ds(t * 8, 8)] = jnp.zeros((8, 32, 128), jnp.bfloat16)
        return carry

    lax.fori_loop(0, buf_ref.shape[0] // 8, clear, 0)

    def block(t, carry):
        for k in range(4):
            n = t * 4 + k
            part = jnp.dot(grid[row_ref[n]], map_ref[n], preferred_element_type=jnp.float32)
            buf_ref[pos_ref[n]] = part.astype(jnp.bfloat16)
        return carry

    lax.fori_loop(0, map_ref.shape[0] // 4, block, 0)


def gather_kernel(target_ref, recv_ref, out_ref, acc):
    acc[...] = jnp.zeros_like(acc)

    def step(t, carry):
        for k in range(4):
            n = t * 4 + k
            c = target_ref[n]
            acc[c] = acc[c] + recv_ref[n].astype(jnp.float32)
        return carry

    lax.fori_loop(0, recv_ref.shape[0] // 4, step, 0)
    out_ref[...] = acc[0 : out_ref.shape[0]].astype(jnp.bfloat16)


def vmem():
    return pl.BlockSpec(memory_space=pltpu.VMEM)


def smem():
    return pl.BlockSpec(memory_space=pltpu.SMEM)


def body(grad_out, pre_act, w_first, w_second, map_blocks, row_block, owner, col_local):
    depth, phi_len, channels, eta = grad_out.shape
    rows = depth * phi_len
    bf16 = jnp.bfloat16
    depth_count = lax.axis_size("depth")
    phi_count = lax.axis_size("phi")
    owners = depth_count * phi_count
    block_count = map_blocks.shape[0]
    cell_size = map_blocks.shape[2]
    slots = max(2, 2 * block_count // owners)
    places = owners * slots
    padded = (depth + 2, (phi_len + 2) * channels, eta)

    low = shift(grad_out[:, -1], "phi", 1, True)
    high = shift(grad_out[:, 0], "phi", -1, True)
    edges = edges_of(grad_out[0], grad_out[-1])

    owner_ids = owner[:, 0]
    count = jnp.arange(block_count, dtype=jnp.int32)
    same = (owner_ids[:, None] == owner_ids[None, :]) & (count[None, :] < count[:, None])
    slot_index = jnp.sum(same.astype(jnp.int32), axis=1)
    owner_depth = owner_ids // phi_count
    owner_phi = owner_ids - owner_depth * phi_count
    position = (owner_phi * depth_count + owner_depth) * slots + slot_index
    taken = position[:, None] == jnp.arange(places, dtype=jnp.int32)[None, :]
    slot_cells = jnp.sum(
        jnp.where(taken, col_local.astype(jnp.float32)[:, None] + 1.0, 0.0), axis=0
    )
    got_cells = lax.all_to_all(
        slot_cells.reshape(phi_count, depth_count * slots), "phi", 0, 0, tiled=True
    )
    cells = got_cells.reshape(phi_count, depth_count, slots).astype(jnp.int32)
    base = (jnp.arange(depth_count, dtype=jnp.int32) * CB_DEV)[None, :, None]
    target = jnp.where(cells > 0, base + cells - 1, depth_count * CB_DEV).reshape(places)

    mix_second = mixing(w_second, phi_len)
    mix_first = mixing(w_first, phi_len)
    grad_rows = grad_out.reshape(rows, channels, eta)
    pre_rows = pre_act.reshape(rows, channels, eta)
    face = jax.ShapeDtypeStruct((depth, channels, eta), bf16)
    hidden, face_first, face_last = pl.pallas_call(
        first_kernel,
        out_shape=(jax.ShapeDtypeStruct((rows, channels, eta), bf16), face, face),
        in_specs=[vmem()] * 6,
        out_specs=(vmem(),) * 3,
        scratch_shapes=[pltpu.VMEM(padded, bf16)],
        compiler_params=pltpu.CompilerParams(vmem_limit_bytes=VMEM_LIMIT),
    )(grad_rows, low, high, edges, pre_rows, mix_second)

    hid_low = shift(face_last, "phi", 1, True)
    hid_high = shift(face_first, "phi", -1, True)
    hid_edges = edges_of(hidden[:phi_len], hidden[rows - phi_len :])
    buffer = pl.pallas_call(
        second_kernel,
        out_shape=jax.ShapeDtypeStruct((places, channels, cell_size), bf16),
        in_specs=[smem()] * 2 + [vmem()] * 7,
        out_specs=vmem(),
        scratch_shapes=[pltpu.VMEM(padded, bf16), pltpu.VMEM((rows, channels, eta), bf16)],
        compiler_params=pltpu.CompilerParams(vmem_limit_bytes=VMEM_LIMIT),
    )(row_block, position, hidden, hid_low, hid_high, hid_edges, grad_rows, mix_first, map_blocks)

    received = lax.all_to_all(
        buffer.reshape(phi_count, depth_count * slots, channels, cell_size), "phi", 0, 0, tiled=True
    ).reshape(places, channels, cell_size)
    sums = pl.pallas_call(
        gather_kernel,
        out_shape=jax.ShapeDtypeStruct((depth_count * CB_DEV, channels, cell_size), bf16),
        in_specs=[smem(), vmem()],
        out_specs=vmem(),
        scratch_shapes=[pltpu.VMEM((depth_count * CB_DEV + 1, channels, cell_size), jnp.float32)],
        compiler_params=pltpu.CompilerParams(vmem_limit_bytes=VMEM_LIMIT),
    )(target, received)
    parts = lax.all_to_all(
        sums.reshape(depth_count, CB_DEV, channels, cell_size), "depth", 0, 0, tiled=True
    )
    return jnp.sum(parts.astype(jnp.float32), axis=0)


def solution(mesh):
    return jax.shard_map(
        body,
        mesh=mesh,
        in_specs=(
            P("depth", "phi", None, None),
            P("depth", "phi", None, None),
            P(),
            P(),
            P(("depth", "phi"), None, None),
            P(("depth", "phi")),
            P(("depth", "phi"), None),
            P(("depth", "phi")),
        ),
        out_specs=P(("depth", "phi"), None, None),
        check_vma=False,
    )
```

profile of v0, /device:TPU:2, one launch (start us, length us, event | category | flops | bytes accessed | tf_op | source)
XLA Modules:
  0.0 166.5 jit_solution(8900562922885548647)
XLA Ops:
  0.0 0.8 slice_bitcast_fusion.3
  0.9 3.5 %collective-permute-start.2 = (bf16[4,32,128]{2,1,0:T(8,128)(2,1)S(1)}, bf16[4,32,128]{2,1,0:T(8,128)(2,1)S(1)}, u32[]{:S(2)}, u32[]{:S(2)}) collective-permute-start(bf16[4,32,128]{2,1,0:T(8,128)(2,1)S(1)} %get-tuple-element.13), channel_id=1, source_target_pairs={{0,8},{8,16},{16,24},{1,9},{9,17},{17,25},{2,10},{10,18},{18,26},{... | collective-permute-start | bytes 98312 | tf_op jit(solution)/shard_map/ppermute | solution.py:17
  4.3 1.3 collective-permute-start.3
  5.6 3.1 %slice_bitcast_fusion = (bf16[112,32,128]{2,1,0:T(8,128)(2,1)}, bf16[112,32,128]{2,1,0:T(8,128)(2,1)}) fusion(bf16[112,4,32,128]{3,2,1,0:T(8,128)(2,1)} %param.8), kind=kLoop, calls=%fused_computation | loop fusion | bytes 3670016 | tf_op jit(solution)/shard_map/squeeze | solution.py:163
  8.7 1.7 %collective-permute-start.1 = (bf16[112,32,128]{2,1,0:T(8,128)(2,1)}, bf16[112,32,128]{2,1,0:T(8,128)(2,1)S(1)}, u32[]{:S(2)}, u32[]{:S(2)}) collective-permute-start(bf16[112,32,128]{2,1,0:T(8,128)(2,1)} %get-tuple-element.15), channel_id=1, source_target_pairs={{0,7},{1,0},{2,1},{3,2},{4,3},{5,4},{6,5},{7,6},{8,15},{9,8},{10,9... | collective-permute-start | bytes 2752520 | tf_op jit(solution)/shard_map/ppermute | solution.py:17
  11.5 4.7 %all-to-all-start = ((f32[8,1,32]{2,1,0:T(1,128)}), f32[8,1,32]{2,1,0:T(1,128)S(1)}, u32[]{:S(2)}, u32[]{:S(2)}) async-start(f32[8,1,32]{2,1,0:T(1,128)} %all_to_all.12), calls=%async_computation | async-start | bytes 8192 | tf_op jit(solution)/shard_map/all_to_all | solution.py:177
  17.1 1.6 collective-permute-start.5
  20.1 10.0 %collective-permute-done.4 = bf16[2,32,128]{2,1,0:T(8,128)(2,1)S(1)} collective-permute-done((bf16[2,32,128]{2,1,0:T(8,128)(2,1)S(1)}, bf16[2,32,128]{2,1,0:T(8,128)(2,1)S(1)}, u32[]{:S(2)}, u32[]{:S(2)}) %collective-permute-start.4) | collective-permute-done | bytes 16416 | tf_op jit(solution)/shard_map/ppermute | solution.py:17
  30.2 0.8 collective-permute-done.5
  31.0 28.1 %shard_map.82 = (bf16[448,32,128]{2,1,0:T(8,128)(2,1)}, bf16[112,32,128]{2,1,0:T(8,128)(2,1)S(1)}, bf16[112,32,128]{2,1,0:T(8,128)(2,1)}) custom-call(bf16[448,32,128]{2,1,0:T(8,128)(2,1)} %bitcast.67, bf16[112,32,128]{2,1,0:T(8,128)(2,1)S(1)} %collective-permute-done.low_ref, bf16[112,32,128]{2,1,0:T(8,128)(2,1)S(1)} %collective-permute-done.1.high_ref, ...), custom_call_target="tpu_custom_call" | custom-call | tf_op jit(solution)/shard_map/pallas_call | solution.py:189
  59.1 1.9 %collective-permute-start.6 = (bf16[112,32,128]{2,1,0:T(8,128)(2,1)}, bf16[112,32,128]{2,1,0:T(8,128)(2,1)S(1)}, u32[]{:S(2)}, u32[]{:S(2)}) collective-permute-start(bf16[112,32,128]{2,1,0:T(8,128)(2,1)} %get-tuple-element.9), channel_id=1, source_target_pairs={{0,1},{1,2},{2,3},{3,4},{4,5},{5,6},{6,7},{7,0},{8,9},{9,10},{10,1... | collective-permute-start | bytes 2752520 | tf_op jit(solution)/shard_map/ppermute | solution.py:17
  61.9 4.5 %collective-permute-start.8 = (bf16[4,32,128]{2,1,0:T(8,128)(2,1)S(1)}, bf16[4,32,128]{2,1,0:T(8,128)(2,1)S(1)}, u32[]{:S(2)}, u32[]{:S(2)}) collective-permute-start(bf16[4,32,128]{2,1,0:T(8,128)(2,1)S(1)} %get-tuple-element.11), channel_id=1, source_target_pairs={{0,8},{8,16},{16,24},{1,9},{9,17},{17,25},{2,10},{10,18},{18,26},{... | collective-permute-start | bytes 98312 | tf_op jit(solution)/shard_map/ppermute | solution.py:17
  66.4 1.3 collective-permute-start.9
  68.0 4.2 %collective-permute-done.9 = bf16[4,32,128]{2,1,0:T(8,128)(2,1)S(1)} collective-permute-done((bf16[4,32,128]{2,1,0:T(8,128)(2,1)S(1)}, bf16[4,32,128]{2,1,0:T(8,128)(2,1)S(1)}, u32[]{:S(2)}, u32[]{:S(2)}) %collective-permute-start.9) | collective-permute-done | bytes 32800 | tf_op jit(solution)/shard_map/ppermute | solution.py:17
  72.3 1.7 %collective-permute-start.11 = (bf16[2,32,128]{2,1,0:T(8,128)(2,1)S(1)}, bf16[2,32,128]{2,1,0:T(8,128)(2,1)S(1)}, u32[]{:S(2)}, u32[]{:S(2)}) collective-permute-start(bf16[2,32,128]{2,1,0:T(8,128)(2,1)S(1)} %get-tuple-element.26), channel_id=1, source_target_pairs={{0,7},{1,0},{2,1},{3,2},{4,3},{5,4},{6,5},{7,6},{8,15},{9,8},{10,9... | collective-permute-start | bytes 49160 | tf_op jit(solution)/shard_map/ppermute | solution.py:17
  74.1 1.4 copy.28
  75.6 1.8 %reshape.60.w_ref = bf16[384,576]{1,0:T(8,128)(2,1)S(1)} reshape(bf16[3,4,32,3,192]{4,3,2,1,0:T(4,128)(2,1)} %copy.28) | data formatting | bytes 884736 | tf_op jit(solution)/shard_map/reshape | solution.py:39
  77.3 3.6 %collective-permute-done.10 = bf16[2,32,128]{2,1,0:T(8,128)(2,1)S(1)} collective-permute-done((bf16[2,32,128]{2,1,0:T(8,128)(2,1)S(1)}, bf16[2,32,128]{2,1,0:T(8,128)(2,1)S(1)}, u32[]{:S(2)}, u32[]{:S(2)}) %collective-permute-start.10) | collective-permute-done | bytes 16416 | tf_op jit(solution)/shard_map/ppermute | solution.py:17
  81.0 1.0 collective-permute-done.11
  82.0 33.5 %shard_map.83 = bf16[256,32,128]{2,1,0:T(8,128)(2,1)} custom-call(s32[128]{0:T(128)S(1)} %copy-done, s32[128]{0:T(128)S(1)} %multiply_add_fusion.pos_ref, bf16[448,32,128]{2,1,0:T(8,128)(2,1)} %get-tuple-element.8.x_ref, bf16[112,32,128]{2,1,0:T(8,128)(2,1)S(1)} %collective-permute-done.6.low_ref, bf16[112,32,128]{2,1,0:T(8,128)(2,1)S(1)} %collective-permute-done.7.high_ref, ...), custom_call_target="tpu_custom_call" | custom-call | tf_op jit(solution)/shard_map/pallas_call | solution.py:201
  115.5 5.5 %all-to-all-start.1 = ((bf16[8,32,32,128]{3,2,1,0:T(8,128)(2,1)}), bf16[8,32,32,128]{3,2,1,0:T(8,128)(2,1)S(1)}, u32[]{:S(2)}, u32[]{:S(2)}) async-start(bf16[8,32,32,128]{3,2,1,0:T(8,128)(2,1)} %bitcast.31), calls=%async_computation.1 | async-start | bytes 4194304 | tf_op jit(solution)/shard_map/all_to_all | solution.py:210
  121.3 24.9 %all-to-all-done.1 = bf16[8,32,32,128]{3,2,1,0:T(8,128)(2,1)S(1)} async-done(((bf16[8,32,32,128]{3,2,1,0:T(8,128)(2,1)}), bf16[8,32,32,128]{3,2,1,0:T(8,128)(2,1)S(1)}, u32[]{:S(2)}, u32[]{:S(2)}) %all-to-all-start.1) | async-done | bytes 2097184 | tf_op jit(solution)/shard_map/all_to_all | solution.py:210
  146.1 1.9 %shard_map.84 = bf16[48,32,128]{2,1,0:T(8,128)(2,1)S(1)} custom-call(s32[256]{0:T(256)S(1)} %compare_select_fusion.target_ref, bf16[256,32,128]{2,1,0:T(8,128)(2,1)S(1)} %bitcast.65), custom_call_target="tpu_custom_call" | custom-call | tf_op jit(solution)/shard_map/pallas_call | solution.py:213
  148.0 17.8 %all_to_all.19 = bf16[4,12,32,128]{3,2,1,0:T(8,128)(2,1)S(1)} all-to-all(bf16[4,12,32,128]{3,2,1,0:T(8,128)(2,1)S(1)} %bitcast.66), channel_id=1, replica_groups=mesh['depth'=4,'phi'=8] {'depth'}, dimensions={0} | all-to-all | bytes 786432 | tf_op jit(solution)/shard_map/all_to_all | solution.py:221
  (52 shorter events, 5.7 us)
Async XLA Ops:
  0.0 10.4 %copy-start.4 = (s32[128,1]{0,1:T(1,128)S(1)}, s32[128,1]{0,1:T(1,128)}, u32[]{:S(2)}) copy-start(s32[128,1]{0,1:T(1,128)} %param.14) | copy-start | bytes 1540
  0.0 10.6 %copy-start.3 = (s32[128]{0:T(128)S(1)}, s32[128]{0:T(128)}, u32[]{:S(2)}) copy-start(s32[128]{0:T(128)} %param.15) | copy-start | bytes 1540
  0.0 16.1 %copy-start.1 = (bf16[3,3,3,32,32]{4,3,2,1,0:T(8,128)(2,1)S(1)}, bf16[3,3,3,32,32]{4,3,2,1,0:T(8,128)(2,1)}, u32[]{:S(2)}) copy-start(bf16[3,3,3,32,32]{4,3,2,1,0:T(8,128)(2,1)} %param.11) | copy-start | bytes 165892
  0.0 18.6 %copy-start.2 = (bf16[3,3,3,32,32]{4,3,2,1,0:T(8,128)(2,1)S(1)}, bf16[3,3,3,32,32]{4,3,2,1,0:T(8,128)(2,1)}, u32[]{:S(2)}) copy-start(bf16[3,3,3,32,32]{4,3,2,1,0:T(8,128)(2,1)} %param.10) | copy-start | bytes 165892
  0.9 16.0 %collective-permute-start.2 = (bf16[4,32,128]{2,1,0:T(8,128)(2,1)S(1)}, bf16[4,32,128]{2,1,0:T(8,128)(2,1)S(1)}, u32[]{:S(2)}, u32[]{:S(2)}) collective-permute-start(bf16[4,32,128]{2,1,0:T(8,128)(2,1)S(1)} %get-tuple-element.13), channel_id=1, source_target_pairs={{0,8},{8,16},{16,24},{1,9},{9,17},{17,25},{2,10},{10,18},{18,26},{... | collective-permute-start | bytes 98312 | tf_op jit(solution)/shard_map/ppermute | solution.py:17
  4.3 12.5 %collective-permute-start.3 = (bf16[4,32,128]{2,1,0:T(8,128)(2,1)S(1)}, bf16[4,32,128]{2,1,0:T(8,128)(2,1)S(1)}, u32[]{:S(2)}, u32[]{:S(2)}) collective-permute-start(bf16[4,32,128]{2,1,0:T(8,128)(2,1)S(1)} %get-tuple-element.14), channel_id=1, source_target_pairs={{8,0},{16,8},{24,16},{9,1},{17,9},{25,17},{10,2},{18,10},{26,18},{... | collective-permute-start | bytes 98312 | tf_op jit(solution)/shard_map/ppermute | solution.py:17
  8.7 22.3 %collective-permute-start = (bf16[112,32,128]{2,1,0:T(8,128)(2,1)}, bf16[112,32,128]{2,1,0:T(8,128)(2,1)S(1)}, u32[]{:S(2)}, u32[]{:S(2)}) collective-permute-start(bf16[112,32,128]{2,1,0:T(8,128)(2,1)} %get-tuple-element.16), channel_id=1, source_target_pairs={{0,1},{1,2},{2,3},{3,4},{4,5},{5,6},{6,7},{7,0},{8,9},{9,10},{10,1... | collective-permute-start | bytes 2752520 | tf_op jit(solution)/shard_map/ppermute | solution.py:17
  8.7 22.3 %collective-permute-start.1 = (bf16[112,32,128]{2,1,0:T(8,128)(2,1)}, bf16[112,32,128]{2,1,0:T(8,128)(2,1)S(1)}, u32[]{:S(2)}, u32[]{:S(2)}) collective-permute-start(bf16[112,32,128]{2,1,0:T(8,128)(2,1)} %get-tuple-element.15), channel_id=1, source_target_pairs={{0,7},{1,0},{2,1},{3,2},{4,3},{5,4},{6,5},{7,6},{8,15},{9,8},{10,9... | collective-permute-start | bytes 2752520 | tf_op jit(solution)/shard_map/ppermute | solution.py:17
  11.5 104.1 %all-to-all-start = ((f32[8,1,32]{2,1,0:T(1,128)}), f32[8,1,32]{2,1,0:T(1,128)S(1)}, u32[]{:S(2)}, u32[]{:S(2)}) async-start(f32[8,1,32]{2,1,0:T(1,128)} %all_to_all.12), calls=%async_computation | async-start | bytes 8192 | tf_op jit(solution)/shard_map/all_to_all | solution.py:177
  16.9 13.3 %collective-permute-start.4 = (bf16[2,32,128]{2,1,0:T(8,128)(2,1)S(1)}, bf16[2,32,128]{2,1,0:T(8,128)(2,1)S(1)}, u32[]{:S(2)}, u32[]{:S(2)}) collective-permute-start(bf16[2,32,128]{2,1,0:T(8,128)(2,1)S(1)} %get-tuple-element.27), channel_id=1, source_target_pairs={{0,1},{1,2},{2,3},{3,4},{4,5},{5,6},{6,7},{7,0},{8,9},{9,10},{10,1... | collective-permute-start | bytes 49160 | tf_op jit(solution)/shard_map/ppermute | solution.py:17
  17.1 13.9 %collective-permute-start.5 = (bf16[2,32,128]{2,1,0:T(8,128)(2,1)S(1)}, bf16[2,32,128]{2,1,0:T(8,128)(2,1)S(1)}, u32[]{:S(2)}, u32[]{:S(2)}) collective-permute-start(bf16[2,32,128]{2,1,0:T(8,128)(2,1)S(1)} %get-tuple-element.28), channel_id=1, source_target_pairs={{0,7},{1,0},{2,1},{3,2},{4,3},{5,4},{6,5},{7,6},{8,15},{9,8},{10,9... | collective-permute-start | bytes 49160 | tf_op jit(solution)/shard_map/ppermute | solution.py:17
  59.1 22.9 %copy-start = (s32[128]{0:T(128)S(1)}, s32[128]{0:T(128)}, u32[]{:S(2)}) copy-start(s32[128]{0:T(128)} %row_ref.1) | copy-start | bytes 1540
  59.1 22.9 %collective-permute-start.6 = (bf16[112,32,128]{2,1,0:T(8,128)(2,1)}, bf16[112,32,128]{2,1,0:T(8,128)(2,1)S(1)}, u32[]{:S(2)}, u32[]{:S(2)}) collective-permute-start(bf16[112,32,128]{2,1,0:T(8,128)(2,1)} %get-tuple-element.9), channel_id=1, source_target_pairs={{0,1},{1,2},{2,3},{3,4},{4,5},{5,6},{6,7},{7,0},{8,9},{9,10},{10,1... | collective-permute-start | bytes 2752520 | tf_op jit(solution)/shard_map/ppermute | solution.py:17
  61.0 21.0 %collective-permute-start.7 = (bf16[112,32,128]{2,1,0:T(8,128)(2,1)S(1)}, bf16[112,32,128]{2,1,0:T(8,128)(2,1)S(1)}, u32[]{:S(2)}, u32[]{:S(2)}) collective-permute-start(bf16[112,32,128]{2,1,0:T(8,128)(2,1)S(1)} %get-tuple-element.10), channel_id=1, source_target_pairs={{0,7},{1,0},{2,1},{3,2},{4,3},{5,4},{6,5},{7,6},{8,15},{9,8},{10,9... | collective-permute-start | bytes 2752520 | tf_op jit(solution)/shard_map/ppermute | solution.py:17
  61.9 6.1 %collective-permute-start.8 = (bf16[4,32,128]{2,1,0:T(8,128)(2,1)S(1)}, bf16[4,32,128]{2,1,0:T(8,128)(2,1)S(1)}, u32[]{:S(2)}, u32[]{:S(2)}) collective-permute-start(bf16[4,32,128]{2,1,0:T(8,128)(2,1)S(1)} %get-tuple-element.11), channel_id=1, source_target_pairs={{0,8},{8,16},{16,24},{1,9},{9,17},{17,25},{2,10},{10,18},{18,26},{... | collective-permute-start | bytes 98312 | tf_op jit(solution)/shard_map/ppermute | solution.py:17
  66.4 5.8 %collective-permute-start.9 = (bf16[4,32,128]{2,1,0:T(8,128)(2,1)S(1)}, bf16[4,32,128]{2,1,0:T(8,128)(2,1)S(1)}, u32[]{:S(2)}, u32[]{:S(2)}) collective-permute-start(bf16[4,32,128]{2,1,0:T(8,128)(2,1)S(1)} %get-tuple-element.12), channel_id=1, source_target_pairs={{8,0},{16,8},{24,16},{9,1},{17,9},{25,17},{10,2},{18,10},{26,18},{... | collective-permute-start | bytes 98312 | tf_op jit(solution)/shard_map/ppermute | solution.py:17
  72.3 8.7 %collective-permute-start.10 = (bf16[2,32,128]{2,1,0:T(8,128)(2,1)S(1)}, bf16[2,32,128]{2,1,0:T(8,128)(2,1)S(1)}, u32[]{:S(2)}, u32[]{:S(2)}) collective-permute-start(bf16[2,32,128]{2,1,0:T(8,128)(2,1)S(1)} %get-tuple-element.25), channel_id=1, source_target_pairs={{0,1},{1,2},{2,3},{3,4},{4,5},{5,6},{6,7},{7,0},{8,9},{9,10},{10,1... | collective-permute-start | bytes 49160 | tf_op jit(solution)/shard_map/ppermute | solution.py:17
  72.3 9.7 %collective-permute-start.11 = (bf16[2,32,128]{2,1,0:T(8,128)(2,1)S(1)}, bf16[2,32,128]{2,1,0:T(8,128)(2,1)S(1)}, u32[]{:S(2)}, u32[]{:S(2)}) collective-permute-start(bf16[2,32,128]{2,1,0:T(8,128)(2,1)S(1)} %get-tuple-element.26), channel_id=1, source_target_pairs={{0,7},{1,0},{2,1},{3,2},{4,3},{5,4},{6,5},{7,6},{8,15},{9,8},{10,9... | collective-permute-start | bytes 49160 | tf_op jit(solution)/shard_map/ppermute | solution.py:17
  115.5 30.6 %all-to-all-start.1 = ((bf16[8,32,32,128]{3,2,1,0:T(8,128)(2,1)}), bf16[8,32,32,128]{3,2,1,0:T(8,128)(2,1)S(1)}, u32[]{:S(2)}, u32[]{:S(2)}) async-start(bf16[8,32,32,128]{3,2,1,0:T(8,128)(2,1)} %bitcast.31), calls=%async_computation.1 | async-start | bytes 4194304 | tf_op jit(solution)/shard_map/all_to_all | solution.py:210
where the time goes:
time: 167 us; the launch traced here: 166 us
  Pallas kernels  63.5 us (38%)
  waiting for transfers between devices  44.6 us (27%)
  starting transfers between devices  28 us (17%)
  blocking collectives  17.8 us (11%)
  local copies, waits for them, and re-layouts  11 us (7%)
    pallas_call x1, Pallas kernels, body(): pl.pallas_call(second_kernel, out_shape=jax.ShapeDtypeStruct((places, cha...  33.5 us
    pallas_call x1, Pallas kernels, body(): pl.pallas_call(first_kernel, out_shape=(jax.ShapeDtypeStruct((rows, chann...  28.1 us
    all_to_all x1, waiting for transfers between devices, body(): lax.all_to_all(buffer.reshape(phi_count, depth_count * slots, channels, c...  24.9 us
    ppermute x12, waiting for transfers between devices, shift(): return lax.ppermute(block, axis, pairs)  19.8 us
    ppermute x12, starting transfers between devices, shift(): return lax.ppermute(block, axis, pairs)  17.9 us
    all_to_all x1, blocking collectives, body(): lax.all_to_all(sums.reshape(depth_count, CB_DEV, channels, cell_size), 'd...  17.8 us
    all_to_all x1, starting transfers between devices, body(): lax.all_to_all(buffer.reshape(phi_count, depth_count * slots, channels, c...  5.45 us
    all_to_all x1, starting transfers between devices, body(): lax.all_to_all(slot_cells.reshape(phi_count, depth_count * slots), 'phi',...  4.65 us
  transfers between devices with their start and end apart: 14, of which 7 were waited for; matrix products, arithmetic and copies ran while one was open for 6% of the time, Pallas kernels for 37%

commit v1 on v0

--- a/solution.py
+++ b/solution.py
@@ -25,6 +25,27 @@
     corner_high = shift(layers[:, 0], "phi", -1, True)
     middle = layers.reshape(2, -1, layers.shape[-1])
     return jnp.concatenate([corner_low, middle, corner_high], axis=1)
+
+
+def diagonal(block, depth_step, phi_step):
+    depths, phis = lax.axis_size("depth"), lax.axis_size("phi")
+    pairs = [
+        (d * phis + p, (d + depth_step) * phis + (p + phi_step) % phis)
+        for d in range(depths)
+        for p in range(phis)
+        if 0 <= d + depth_step < depths
+    ]
+    return lax.ppermute(block, ("depth", "phi"), pairs)
+
+
+def direct_edges(first_layer, last_layer):
+    sides = []
+    for layer, step in ((last_layer, 1), (first_layer, -1)):
+        low = diagonal(layer[-1], step, 1)
+        high = diagonal(layer[0], step, -1)
+        middle = shift(layer, "depth", step, False).reshape(-1, layer.shape[-1])
+        sides.append(jnp.concatenate([low, middle, high]))
+    return jnp.stack(sides)
 
 
 def mixing(weight, phi_len):
@@ -39,20 +60,25 @@
     return full.reshape(3 * phi_len * channels, 3 * (phi_len + 2) * channels)
 
 
-def fill(xp, x_ref, low_ref, high_ref, edge_ref):
-    depth = low_ref.shape[0]
-    xp[0] = edge_ref[0]
-    xp[depth + 1] = edge_ref[1]
-
-    def step(z, carry):
-        for k in range(4):
-            d = z * 4 + k
-            xp[d + 1, 0:32] = low_ref[d]
-            xp[d + 1, 32:160] = x_ref[pl.ds(d * 4, 4)].reshape(128, 128)
-            xp[d + 1, 160:192] = high_ref[d]
-        return carry
-
-    lax.fori_loop(0, depth // 4, step, 0)
+def fill(xp, pieces):
+    for x_ref, low_ref, high_ref, at, face_at, cells, to in pieces:
+
+        def step(d, x_ref=x_ref, low_ref=low_ref, high_ref=high_ref, at=at, face_at=face_at, to=to):
+            xp[to + d, 0:32] = low_ref[face_at + d]
+            xp[to + d, 32:160] = x_ref[pl.ds((at + d) * 4, 4)].reshape(128, 128)
+            xp[to + d, 160:192] = high_ref[face_at + d]
+
+        whole = cells // 4 * 4
+        if whole:
+
+            def steps(t, carry, step=step):
+                for k in range(4):
+                    step(t * 4 + k)
+                return carry
+
+            lax.fori_loop(0, whole // 4, steps, 0)
+        for d in range(whole, cells):
+            step(d)
 
 
 def conv_pair(xp, w_ref, z):
@@ -75,38 +101,99 @@
     return outs
 
 
-def first_kernel(x_ref, low_ref, high_ref, edge_ref, pre_ref, w_ref, hid_ref, f0_ref, f3_ref, xp):
-    fill(xp, x_ref, low_ref, high_ref, edge_ref)
-    depth = low_ref.shape[0]
-
+def convolve(xp, w_ref, cells, jump_at, jump_xp, depth_at, jump_depth, store):
     def step(t, carry):
-        z = t * 2
-        for k, back in enumerate(conv_pair(xp, w_ref, z)):
-            p = pre_ref[pl.ds((z + k) * 4, 4)].reshape(128, 128).astype(jnp.float32)
-            s = 1.0 / (1.0 + jnp.exp(-p))
-            hid = (back * s * (1.0 + p * (1.0 - s))).astype(jnp.bfloat16)
-            hid_ref[pl.ds((z + k) * 4, 4)] = hid.reshape(4, 32, 128)
-            f0_ref[z + k] = hid[0:32]
-            f3_ref[z + k] = hid[96:128]
-        return carry
-
-    lax.fori_loop(0, depth // 2, step, 0)
-
-
-def second_kernel(
-    row_ref, pos_ref, x_ref, low_ref, high_ref, edge_ref, grad_ref, w_ref, map_ref, buf_ref, xp, grid
+        at = t * 2
+        past = jnp.where(at >= jump_at, 1, 0)
+        base = at + past * jump_xp
+        z = at + depth_at + past * jump_depth
+        for k, back in enumerate(conv_pair(xp, w_ref, base)):
+            store(back, z + k, at + k)
+        return carry
+
+    lax.fori_loop(0, cells // 2, step, 0, unroll=4)
+
+
+def store_hidden(pre_ref, hid_ref, f0_ref, f3_ref):
+    def store(back, z, at):
+        p = pre_ref[pl.ds(z * 4, 4)].reshape(128, 128).astype(jnp.float32)
+        s = 1.0 / (1.0 + jnp.exp(-p))
+        hid = (back * s * (1.0 + p * (1.0 - s))).astype(jnp.bfloat16)
+        hid_ref[pl.ds(at * 4, 4)] = hid.reshape(4, 32, 128)
+        f0_ref[at] = hid[0:32]
+        f3_ref[at] = hid[96:128]
+
+    return store
+
+
+def first_middle(x, low, high, pre, w_ref, hid_ref, f0_ref, f3_ref, xp):
+    depth = x.shape[0] // 4
+    q = depth // 4
+    fill(xp, [(x, low, high, q - 1, 0, depth - 2 * q + 2, 0)])
+    m = depth - 2 * q
+    convolve(xp, w_ref, m, m, 0, q, 0, store_hidden(pre, hid_ref, f0_ref, f3_ref))
+
+
+def first_outer(after, x, low_m, high_m, low, high, edge, pre, w_ref, hid_ref, f0_ref, f3_ref, xp):
+    depth = x.shape[0] // 4
+    q = depth // 4
+    m = depth - 2 * q + 2
+    xp[0] = edge[0]
+    xp[2 * q + 3] = edge[1]
+    fill(
+        xp,
+        [
+            (x, low, high, 0, 0, q - 1, 1),
+            (x, low_m, high_m, q - 1, 0, 2, q),
+            (x, low_m, high_m, depth - q - 1, m - 2, 2, q + 2),
+            (x, low, high, depth - q + 1, q - 1, q - 1, q + 4),
+        ],
+    )
+    store = store_hidden(pre, hid_ref, f0_ref, f3_ref)
+    convolve(xp, w_ref, 2 * q, q, 2, 0, depth - 2 * q, store)
+
+
+def second_middle(after, x, low, high, grad, w_ref, out_ref, xp):
+    mid = x.shape[0] // 4
+    q = mid // 2
+    fill(xp, [(x, low, high, 3, 3, mid - 6, 0)])
+
+    def store(back, z, at):
+        g = grad[pl.ds(z * 4, 4)].reshape(128, 128).astype(jnp.float32)
+        out_ref[pl.ds(at * 4, 4)] = (back + g).astype(jnp.bfloat16).reshape(4, 32, 128)
+
+    convolve(xp, w_ref, mid - 8, mid, 0, q + 4, 0, store)
+
+
+def second_outer(
+    row_ref, pos_ref, x, low, high, x_m, low_m, high_m, edge, grad, mid_ref, w_ref, map_ref, buf_ref, xp, grid
 ):
-    fill(xp, x_ref, low_ref, high_ref, edge_ref)
-    depth = low_ref.shape[0]
-
-    def step(t, carry):
-        z = t * 2
-        for k, back in enumerate(conv_pair(xp, w_ref, z)):
-            g = grad_ref[pl.ds((z + k) * 4, 4)].reshape(128, 128).astype(jnp.float32)
-            grid[pl.ds((z + k) * 4, 4)] = (back + g).astype(jnp.bfloat16).reshape(4, 32, 128)
-        return carry
-
-    lax.fori_loop(0, depth // 2, step, 0)
+    q = x.shape[0] // 8
+    depth = grad.shape[0] // 4
+    m = depth - 2 * q
+    xp[0] = edge[0]
+    xp[2 * q + 11] = edge[1]
+    fill(
+        xp,
+        [
+            (x, low, high, 0, 0, q, 1),
+            (x_m, low_m, high_m, 0, 0, 5, q + 1),
+            (x_m, low_m, high_m, m - 5, m - 5, 5, q + 6),
+            (x, low, high, q, q, q, q + 11),
+        ],
+    )
+
+    def store(back, z, at):
+        g = grad[pl.ds(z * 4, 4)].reshape(128, 128).astype(jnp.float32)
+        grid[pl.ds(z * 4, 4)] = (back + g).astype(jnp.bfloat16).reshape(4, 32, 128)
+
+    convolve(xp, w_ref, 2 * q + 8, q + 4, 2, 0, depth - 2 * q - 8, store)
+
+    def keep(t, carry):
+        grid[pl.ds((q + 4) * 4 + t * 16, 16)] = mid_ref[pl.ds(t * 16, 16)]
+        return carry
+
+    lax.fori_loop(0, mid_ref.shape[0] // 16, keep, 0)
 
     def clear(t, carry):
         buf_ref[pl.ds(t * 8, 8)] = jnp.zeros((8, 32, 128), jnp.bfloat16)
@@ -115,13 +202,13 @@
     lax.fori_loop(0, buf_ref.shape[0] // 8, clear, 0)
 
     def block(t, carry):
-        for k in range(4):
-            n = t * 4 + k
+        for k in range(8):
+            n = t * 8 + k
             part = jnp.dot(grid[row_ref[n]], map_ref[n], preferred_element_type=jnp.float32)
             buf_ref[pos_ref[n]] = part.astype(jnp.bfloat16)
         return carry
 
-    lax.fori_loop(0, map_ref.shape[0] // 4, block, 0)
+    lax.fori_loop(0, map_ref.shape[0] // 8, block, 0, unroll=2)
 
 
 def gather_kernel(target_ref, recv_ref, out_ref, acc):
@@ -144,6 +231,22 @@
 
 def smem():
     return pl.BlockSpec(memory_space=pltpu.SMEM)
+
+
+def kernel(run, arrays, outs, scratch, cells, scalars=0, ordered=0):
+    return pl.pallas_call(
+        run,
+        out_shape=outs,
+        in_specs=[smem()] * scalars
+        + [pl.BlockSpec(memory_space=pl.ANY)] * ordered
+        + [vmem()] * arrays,
+        out_specs=tuple(vmem() for _ in outs) if isinstance(outs, tuple) else vmem(),
+        scratch_shapes=scratch,
+        compiler_params=pltpu.CompilerParams(vmem_limit_bytes=VMEM_LIMIT),
+        cost_estimate=pl.CostEstimate(
+            flops=cells * 2 * 128 * 384 * 576, bytes_accessed=cells * 131072, transcendentals=0
+        ),
+    )
 
 
 def body(grad_out, pre_act, w_first, w_second, map_blocks, row_block, owner, col_local):
@@ -157,10 +260,19 @@
     cell_size = map_blocks.shape[2]
     slots = max(2, 2 * block_count // owners)
     places = owners * slots
-    padded = (depth + 2, (phi_len + 2) * channels, eta)
-
-    low = shift(grad_out[:, -1], "phi", 1, True)
-    high = shift(grad_out[:, 0], "phi", -1, True)
+    q = depth // 4
+    middle = depth - 2 * q
+
+    def padded(cells):
+        return pltpu.VMEM((cells, (phi_len + 2) * channels, eta), bf16)
+
+    def outer_face(phi_at):
+        return jnp.concatenate([grad_out[: q - 1, phi_at], grad_out[depth - q + 1 :, phi_at]])
+
+    low_m = shift(grad_out[q - 1 : depth - q + 1, -1], "phi", 1, True)
+    high_m = shift(grad_out[q - 1 : depth - q + 1, 0], "phi", -1, True)
+    low_o = shift(outer_face(phi_len - 1), "phi", 1, True)
+    high_o = shift(outer_face(0), "phi", -1, True)
     edges = edges_of(grad_out[0], grad_out[-1])
 
     owner_ids = owner[:, 0]
@@ -185,27 +297,37 @@
     mix_first = mixing(w_first, phi_len)
     grad_rows = grad_out.reshape(rows, channels, eta)
     pre_rows = pre_act.reshape(rows, channels, eta)
-    face = jax.ShapeDtypeStruct((depth, channels, eta), bf16)
-    hidden, face_first, face_last = pl.pallas_call(
-        first_kernel,
-        out_shape=(jax.ShapeDtypeStruct((rows, channels, eta), bf16), face, face),
-        in_specs=[vmem()] * 6,
-        out_specs=(vmem(),) * 3,
-        scratch_shapes=[pltpu.VMEM(padded, bf16)],
-        compiler_params=pltpu.CompilerParams(vmem_limit_bytes=VMEM_LIMIT),
-    )(grad_rows, low, high, edges, pre_rows, mix_second)
-
-    hid_low = shift(face_last, "phi", 1, True)
-    hid_high = shift(face_first, "phi", -1, True)
-    hid_edges = edges_of(hidden[:phi_len], hidden[rows - phi_len :])
-    buffer = pl.pallas_call(
-        second_kernel,
-        out_shape=jax.ShapeDtypeStruct((places, channels, cell_size), bf16),
-        in_specs=[smem()] * 2 + [vmem()] * 7,
-        out_specs=vmem(),
-        scratch_shapes=[pltpu.VMEM(padded, bf16), pltpu.VMEM((rows, channels, eta), bf16)],
-        compiler_params=pltpu.CompilerParams(vmem_limit_bytes=VMEM_LIMIT),
-    )(row_block, position, hidden, hid_low, hid_high, hid_edges, grad_rows, mix_first, map_blocks)
+    def array(cells):
+        return jax.ShapeDtypeStruct((cells, channels, eta), bf16)
+
+    def hidden_outs(cells):
+        return array(cells * phi_len), array(cells), array(cells)
+
+    hid_m, hid_m0, hid_m3 = kernel(
+        first_middle, 5, hidden_outs(middle), [padded(middle + 2)], middle
+    )(grad_rows, low_m, high_m, pre_rows, mix_second)
+    hid_low_m = shift(hid_m3, "phi", 1, True)
+    hid_high_m = shift(hid_m0, "phi", -1, True)
+    hid_o, hid_o0, hid_o3 = kernel(
+        first_outer, 8, hidden_outs(2 * q), [padded(2 * q + 4)], 2 * q, ordered=1
+    )(hid_m0, grad_rows, low_m, high_m, low_o, high_o, edges, pre_rows, mix_second)
+    hid_low_o = shift(hid_o3, "phi", 1, True)
+    hid_high_o = shift(hid_o0, "phi", -1, True)
+    hid_edges = direct_edges(hid_o[:phi_len], hid_o[(2 * q - 1) * phi_len :])
+    grid_m = kernel(
+        second_middle, 5, array((middle - 8) * phi_len), [padded(middle - 6)], middle - 8, ordered=1
+    )(hid_o0, hid_m, hid_low_m, hid_high_m, grad_rows, mix_first)
+    buffer = kernel(
+        second_outer,
+        11,
+        array(places),
+        [padded(2 * q + 12), pltpu.VMEM((rows, channels, eta), bf16)],
+        2 * q + 8,
+        scalars=2,
+    )(
+        row_block, position, hid_o, hid_low_o, hid_high_o, hid_m, hid_low_m, hid_high_m,
+        hid_edges, grad_rows, grid_m, mix_first, map_blocks,
+    )
 
     received = lax.all_to_all(
         buffer.reshape(phi_count, depth_count * slots, channels, cell_size), "phi", 0, 0, tiled=True

time: 167 us -> 163 us (0.976)
  Pallas kernels: 63.5 us -> 45.2 us
  waiting for transfers between devices: 44.6 us -> 31.5 us
  local copies, waits for them, and re-layouts: 11 us -> 23.1 us
  starting transfers between devices: 28 us -> 37.3 us
  other arithmetic: 1.37 us -> 5.52 us
    pallas_call x2 -> x4, Pallas kernels: 61.6 us -> 43.4 us  [the longest x1 15 us: body(): kernel(second_outer, 11, array(places), [padded(2 * q + 12), pltpu.VMEM((...]
    ppermute x12 -> x14, waiting for transfers between devices: 19.8 us -> 3.49 us  [shift(): return lax.ppermute(block, axis, pairs)]
    ppermute x0 -> x4, starting transfers between devices: none -> 11.2 us  [diagonal(): return lax.ppermute(block, ('depth', 'phi'), pairs)]
    unnamed x10 -> x46, local copies, waits for them, and re-layouts: 0.02 us -> 7.68 us
    ppermute x0 -> x4, waiting for transfers between devices: none -> 3.19 us  [diagonal(): return lax.ppermute(block, ('depth', 'phi'), pairs)]
    another operation x4, local copies, waits for them, and re-layouts: 2.35 us -> 4.67 us  [mixing(): full = jnp.stack(rows, axis=1)]
    ppermute x12 -> x14, starting transfers between devices: 17.9 us -> 16.3 us  [shift(): return lax.ppermute(block, axis, pairs)]
    squeeze x1 -> x3, local copies, waits for them, and re-layouts: 3.06 us -> 4.26 us  [the longest x1 2.23 us: body(): high_m = shift(grad_out[q - 1:depth - q + 1, 0], 'phi', -1, True)]
  transfers between devices with their start and end apart: 14 -> 20, of which waited for: 7 -> 6; matrix products, arithmetic and copies ran while one was open for 6% -> 11% of each run, Pallas kernels for 37% -> 27%
where the time goes in v1:
time: 163 us; the launch traced here: 162 us
  Pallas kernels  45.2 us (28%)
  starting transfers between devices  37.3 us (23%)
  waiting for transfers between devices  31.5 us (19%)
  local copies, waits for them, and re-layouts  23.1 us (14%)
  blocking collectives  18.7 us (11%)
  other arithmetic  5.52 us (3%)
    all_to_all x1, waiting for transfers between devices, body(): lax.all_to_all(buffer.reshape(phi_count, depth_count * slots, channels, c...  24.9 us
    all_to_all x1, blocking collectives, body(): lax.all_to_all(sums.reshape(depth_count, CB_DEV, channels, cell_size), 'd...  18.7 us
    ppermute x14, starting transfers between devices, shift(): return lax.ppermute(block, axis, pairs)  16.3 us
    pallas_call x1, Pallas kernels, body(): kernel(second_outer, 11, array(places), [padded(2 * q + 12), pltpu.VMEM((...  15 us
    ppermute x4, starting transfers between devices, diagonal(): return lax.ppermute(block, ('depth', 'phi'), pairs)  11.2 us
    pallas_call x1, Pallas kernels, body(): kernel(first_middle, 5, hidden_outs(middle), [padded(middle + 2)], middle)  11 us
    pallas_call x1, Pallas kernels, body(): kernel(first_outer, 8, hidden_outs(2 * q), [padded(2 * q + 4)], 2 * q, or...  9.77 us
    unnamed x46, local copies, waits for them, and re-layouts  7.68 us
  transfers between devices with their start and end apart: 20, of which 6 were waited for; matrix products, arithmetic and copies ran while one was open for 11% of the time, Pallas kernels for 27%

profile of v1, /device:TPU:2, one launch (start us, length us, event | category | flops | bytes accessed | tf_op | source)
XLA Modules:
  0.0 161.9 jit_solution(11382421857885259248)
XLA Ops:
  0.0 2.2 %slice_bitcast_fusion = (bf16[58,32,128]{2,1,0:T(8,128)(2,1)}, bf16[58,32,128]{2,1,0:T(8,128)(2,1)}) fusion(bf16[112,4,32,128]{3,2,1,0:T(8,128)(2,1)} %param.8), kind=kLoop, calls=%fused_computation.3 | loop fusion | bytes 1900544 | tf_op jit(solution)/shard_map/squeeze | solution.py:273
  2.2 1.7 %collective-permute-start.1 = (bf16[58,32,128]{2,1,0:T(8,128)(2,1)}, bf16[58,32,128]{2,1,0:T(8,128)(2,1)S(1)}, u32[]{:S(2)}, u32[]{:S(2)}) collective-permute-start(bf16[58,32,128]{2,1,0:T(8,128)(2,1)} %get-tuple-element.23), channel_id=1, source_target_pairs={{0,7},{1,0},{2,1},{3,2},{4,3},{5,4},{6,5},{7,6},{8,15},{9,8},{10,9... | collective-permute-start | bytes 1425416 | tf_op jit(solution)/shard_map/ppermute | solution.py:17
  4.8 3.5 %collective-permute-start.4 = (bf16[4,32,128]{2,1,0:T(8,128)(2,1)S(1)}, bf16[4,32,128]{2,1,0:T(8,128)(2,1)S(1)}, u32[]{:S(2)}, u32[]{:S(2)}) collective-permute-start(bf16[4,32,128]{2,1,0:T(8,128)(2,1)S(1)} %get-tuple-element.17), channel_id=1, source_target_pairs={{0,8},{8,16},{16,24},{1,9},{9,17},{17,25},{2,10},{10,18},{18,26},{... | collective-permute-start | bytes 98312 | tf_op jit(solution)/shard_map/ppermute | solution.py:17
  9.5 1.3 slice_bitcast_fusion.3
  12.7 5.4 %all-to-all-start = ((f32[8,1,32]{2,1,0:T(1,128)}), f32[8,1,32]{2,1,0:T(1,128)S(1)}, u32[]{:S(2)}, u32[]{:S(2)}) async-start(f32[8,1,32]{2,1,0:T(1,128)} %all_to_all.12), calls=%async_computation | async-start | bytes 8192 | tf_op jit(solution)/shard_map/all_to_all | solution.py:289
  22.1 1.9 %collective-permute-done.6 = bf16[2,32,128]{2,1,0:T(8,128)(2,1)S(1)} collective-permute-done((bf16[2,32,128]{2,1,0:T(8,128)(2,1)S(1)}, bf16[2,32,128]{2,1,0:T(8,128)(2,1)S(1)}, u32[]{:S(2)}, u32[]{:S(2)}) %collective-permute-start.6) | collective-permute-done | bytes 16416 | tf_op jit(solution)/shard_map/ppermute | solution.py:17
  25.4 1.4 copy.34
  26.8 1.8 %reshape.59.w_ref = bf16[384,576]{1,0:T(8,128)(2,1)S(1)} reshape(bf16[3,4,32,3,192]{4,3,2,1,0:T(4,128)(2,1)} %copy.34) | data formatting | bytes 884736 | tf_op jit(solution)/shard_map/reshape | solution.py:60
  29.4 11.0 %shard_map.82 = (bf16[224,32,128]{2,1,0:T(8,128)(2,1)S(1)}, bf16[56,32,128]{2,1,0:T(8,128)(2,1)}, bf16[56,32,128]{2,1,0:T(8,128)(2,1)}) custom-call(bf16[448,32,128]{2,1,0:T(8,128)(2,1)} %bitcast.89, bf16[58,32,128]{2,1,0:T(8,128)(2,1)S(1)} %collective-permute-done.low.low_m, bf16[58,32,128]{2,1,0:T(8,128)(2,1)S(1)} %collective-permute-done.1.high.high_m, ...), custom_call_target="tpu_custom_call" | custom-call | flops 3170893824 | bytes 7340032 | tf_op jit(solution)/shard_map/pallas_call | solution.py:306
  41.7 3.6 %collective-permute-start.11 = (bf16[56,32,128]{2,1,0:T(8,128)(2,1)}, bf16[56,32,128]{2,1,0:T(8,128)(2,1)S(1)}, u32[]{:S(2)}, u32[]{:S(2)}) collective-permute-start(bf16[56,32,128]{2,1,0:T(8,128)(2,1)} %get-tuple-element.11.after), channel_id=1, source_target_pairs={{0,7},{1,0},{2,1},{3,2},{4,3},{5,4},{6,5},{7,6},{8,15},{9,8},{10,9... | collective-permute-start | bytes 1376264 | tf_op jit(solution)/shard_map/ppermute | solution.py:17
  49.2 9.8 %shard_map.83 = (bf16[224,32,128]{2,1,0:T(8,128)(2,1)S(1)}, bf16[56,32,128]{2,1,0:T(8,128)(2,1)S(1)}, bf16[56,32,128]{2,1,0:T(8,128)(2,1)S(1)}) custom-call(bf16[56,32,128]{2,1,0:T(8,128)(2,1)} %get-tuple-element.11.after, bf16[448,32,128]{2,1,0:T(8,128)(2,1)} %bitcast.90, bf16[58,32,128]{2,1,0:T(8,128)(2,1)S(1)} %copy-done.4, ...), custom_call_target="tpu_custom_call" | custom-call | flops 3170893824 | bytes 7340032 | tf_op jit(solution)/shard_map/pallas_call | solution.py:311
  60.3 4.6 %collective-permute-start.12 = (bf16[32,128]{1,0:T(8,128)(2,1)}, bf16[32,128]{1,0:T(8,128)(2,1)S(1)}, u32[]{:S(2)}, u32[]{:S(2)}) collective-permute-start(bf16[32,128]{1,0:T(8,128)(2,1)} %get-tuple-element.25), channel_id=1, source_target_pairs={{0,9},{1,10},{2,11},{3,12},{4,13},{5,14},{6,15},{7,8},{8,17},{9,18... | collective-permute-start | bytes 24584 | tf_op jit(solution)/shard_map/ppermute | solution.py:38
  64.9 4.0 %collective-permute-start.14 = (bf16[32,128]{1,0:T(8,128)(2,1)}, bf16[32,128]{1,0:T(8,128)(2,1)S(1)}, u32[]{:S(2)}, u32[]{:S(2)}) collective-permute-start(bf16[32,128]{1,0:T(8,128)(2,1)} %get-tuple-element.28), channel_id=1, source_target_pairs={{0,15},{1,8},{2,9},{3,10},{4,11},{5,12},{6,13},{7,14},{8,23},{9,16... | collective-permute-start | bytes 24584 | tf_op jit(solution)/shard_map/ppermute | solution.py:38
  68.9 4.1 %collective-permute-start.13 = (bf16[4,32,128]{2,1,0:T(8,128)(2,1)}, bf16[4,32,128]{2,1,0:T(8,128)(2,1)}, u32[]{:S(2)}, u32[]{:S(2)}) collective-permute-start(bf16[4,32,128]{2,1,0:T(8,128)(2,1)} %get-tuple-element.29), channel_id=1, source_target_pairs={{0,8},{8,16},{16,24},{1,9},{9,17},{17,25},{2,10},{10,18},{18,26},{... | collective-permute-start | bytes 98312 | tf_op jit(solution)/shard_map/ppermute | solution.py:17
  73.2 1.4 copy.40
  74.6 1.8 %reshape.63.w_ref = bf16[384,576]{1,0:T(8,128)(2,1)S(1)} reshape(bf16[3,4,32,3,192]{4,3,2,1,0:T(4,128)(2,1)} %copy.40) | data formatting | bytes 884736 | tf_op jit(solution)/shard_map/reshape | solution.py:60
  82.3 2.0 %collective-permute-done.17 = bf16[32,128]{1,0:T(8,128)(2,1)S(1)} collective-permute-done((bf16[32,128]{1,0:T(8,128)(2,1)S(1)}, bf16[32,128]{1,0:T(8,128)(2,1)S(1)}, u32[]{:S(2)}, u32[]{:S(2)}) %collective-permute-start.17) | collective-permute-done | bytes 8224 | tf_op jit(solution)/shard_map/ppermute | solution.py:38
  85.5 1.5 copy-done.1
  88.1 7.6 %shard_map.84.mid_ref = bf16[192,32,128]{2,1,0:T(8,128)(2,1)S(1)} custom-call(bf16[56,32,128]{2,1,0:T(8,128)(2,1)S(1)} %copy-done.9, bf16[224,32,128]{2,1,0:T(8,128)(2,1)S(1)} %copy-done.1, bf16[56,32,128]{2,1,0:T(8,128)(2,1)S(1)} %collective-permute-done.10.low.low_m, bf16[56,32,128]{2,1,0:T(8,128)(2,1)S(1)} %collective-permute-done.11.high.high_m, ...), custom_call_target="tpu_custom_call" | custom-call | flops 2717908992 | bytes 6291456 | tf_op jit(solution)/shard_map/pallas_call | solution.py:317
  96.1 15.0 %shard_map.85 = bf16[256,32,128]{2,1,0:T(8,128)(2,1)} custom-call(s32[128]{0:T(128)S(1)} %copy-done.2, s32[128]{0:T(128)S(1)} %multiply_add_fusion.pos_ref, bf16[224,32,128]{2,1,0:T(8,128)(2,1)S(1)} %get-tuple-element.12.x, bf16[56,32,128]{2,1,0:T(8,128)(2,1)S(1)} %collective-permute-done.8.low, bf16[56,32,128]{2,1,0:T(8,128)(2,1)S(1)} %collective-permute-done.9.high, ...), custom_call_target="tpu_custom_call" | custom-call | flops 3623878656 | bytes 8388608 | tf_op jit(solution)/shard_map/pallas_call | solution.py:320
  111.1 4.3 %all-to-all-start.1 = ((bf16[8,32,32,128]{3,2,1,0:T(8,128)(2,1)}), bf16[8,32,32,128]{3,2,1,0:T(8,128)(2,1)S(1)}, u32[]{:S(2)}, u32[]{:S(2)}) async-start(bf16[8,32,32,128]{3,2,1,0:T(8,128)(2,1)} %bitcast.93), calls=%async_computation.1 | async-start | bytes 4194304 | tf_op jit(solution)/shard_map/all_to_all | solution.py:332
  115.7 24.9 %all-to-all-done.1 = bf16[8,32,32,128]{3,2,1,0:T(8,128)(2,1)S(1)} async-done(((bf16[8,32,32,128]{3,2,1,0:T(8,128)(2,1)}), bf16[8,32,32,128]{3,2,1,0:T(8,128)(2,1)S(1)}, u32[]{:S(2)}, u32[]{:S(2)}) %all-to-all-start.1) | async-done | bytes 2097184 | tf_op jit(solution)/shard_map/all_to_all | solution.py:332
  140.6 1.9 %shard_map.86 = bf16[48,32,128]{2,1,0:T(8,128)(2,1)S(1)} custom-call(s32[256]{0:T(256)S(1)} %compare_select_fusion.target_ref, bf16[256,32,128]{2,1,0:T(8,128)(2,1)S(1)} %bitcast.87), custom_call_target="tpu_custom_call" | custom-call | tf_op jit(solution)/shard_map/pallas_call | solution.py:335
  142.5 18.7 %all_to_all.19 = bf16[4,12,32,128]{3,2,1,0:T(8,128)(2,1)S(1)} all-to-all(bf16[4,12,32,128]{3,2,1,0:T(8,128)(2,1)S(1)} %bitcast.88), channel_id=1, replica_groups=mesh['depth'=4,'phi'=8] {'depth'}, dimensions={0} | all-to-all | bytes 786432 | tf_op jit(solution)/shard_map/all_to_all | solution.py:343
  (107 shorter events, 26.0 us)
Async XLA Ops:
  0.0 18.2 %copy-start.14 = (bf16[3,3,3,32,32]{4,3,2,1,0:T(8,128)(2,1)S(1)}, bf16[3,3,3,32,32]{4,3,2,1,0:T(8,128)(2,1)}, u32[]{:S(2)}) copy-start(bf16[3,3,3,32,32]{4,3,2,1,0:T(8,128)(2,1)} %param.11) | copy-start | bytes 165892
  2.2 27.1 %collective-permute-start = (bf16[58,32,128]{2,1,0:T(8,128)(2,1)}, bf16[58,32,128]{2,1,0:T(8,128)(2,1)S(1)}, u32[]{:S(2)}, u32[]{:S(2)}) collective-permute-start(bf16[58,32,128]{2,1,0:T(8,128)(2,1)} %get-tuple-element.24), channel_id=1, source_target_pairs={{0,1},{1,2},{2,3},{3,4},{4,5},{5,6},{6,7},{7,0},{8,9},{9,10},{10,1... | collective-permute-start | bytes 1425416 | tf_op jit(solution)/shard_map/ppermute | solution.py:17
  2.2 27.1 %collective-permute-start.1 = (bf16[58,32,128]{2,1,0:T(8,128)(2,1)}, bf16[58,32,128]{2,1,0:T(8,128)(2,1)S(1)}, u32[]{:S(2)}, u32[]{:S(2)}) collective-permute-start(bf16[58,32,128]{2,1,0:T(8,128)(2,1)} %get-tuple-element.23), channel_id=1, source_target_pairs={{0,7},{1,0},{2,1},{3,2},{4,3},{5,4},{6,5},{7,6},{8,15},{9,8},{10,9... | collective-permute-start | bytes 1425416 | tf_op jit(solution)/shard_map/ppermute | solution.py:17
  4.8 15.8 %collective-permute-start.4 = (bf16[4,32,128]{2,1,0:T(8,128)(2,1)S(1)}, bf16[4,32,128]{2,1,0:T(8,128)(2,1)S(1)}, u32[]{:S(2)}, u32[]{:S(2)}) collective-permute-start(bf16[4,32,128]{2,1,0:T(8,128)(2,1)S(1)} %get-tuple-element.17), channel_id=1, source_target_pairs={{0,8},{8,16},{16,24},{1,9},{9,17},{17,25},{2,10},{10,18},{18,26},{... | collective-permute-start | bytes 98312 | tf_op jit(solution)/shard_map/ppermute | solution.py:17
  8.2 12.5 %collective-permute-start.5 = (bf16[4,32,128]{2,1,0:T(8,128)(2,1)S(1)}, bf16[4,32,128]{2,1,0:T(8,128)(2,1)S(1)}, u32[]{:S(2)}, u32[]{:S(2)}) collective-permute-start(bf16[4,32,128]{2,1,0:T(8,128)(2,1)S(1)} %get-tuple-element.18), channel_id=1, source_target_pairs={{8,0},{16,8},{24,16},{9,1},{17,9},{25,17},{10,2},{18,10},{26,18},{... | collective-permute-start | bytes 98312 | tf_op jit(solution)/shard_map/ppermute | solution.py:17
  11.7 33.6 %collective-permute-start.2 = (bf16[54,32,128]{2,1,0:T(8,128)(2,1)}, bf16[54,32,128]{2,1,0:T(8,128)(2,1)S(1)}, u32[]{:S(2)}, u32[]{:S(2)}) collective-permute-start(bf16[54,32,128]{2,1,0:T(8,128)(2,1)} %pad_maximum_fusion.2), channel_id=1, source_target_pairs={{0,1},{1,2},{2,3},{3,4},{4,5},{5,6},{6,7},{7,0},{8,9},{9,10},{10,1... | collective-permute-start | bytes 1327112 | tf_op jit(solution)/shard_map/ppermute | solution.py:17
  12.7 98.4 %all-to-all-start = ((f32[8,1,32]{2,1,0:T(1,128)}), f32[8,1,32]{2,1,0:T(1,128)S(1)}, u32[]{:S(2)}, u32[]{:S(2)}) async-start(f32[8,1,32]{2,1,0:T(1,128)} %all_to_all.12), calls=%async_computation | async-start | bytes 8192 | tf_op jit(solution)/shard_map/all_to_all | solution.py:289
  20.6 24.7 %collective-permute-start.3 = (bf16[54,32,128]{2,1,0:T(8,128)(2,1)}, bf16[54,32,128]{2,1,0:T(8,128)(2,1)S(1)}, u32[]{:S(2)}, u32[]{:S(2)}) collective-permute-start(bf16[54,32,128]{2,1,0:T(8,128)(2,1)} %pad_maximum_fusion.3), channel_id=1, source_target_pairs={{0,7},{1,0},{2,1},{3,2},{4,3},{5,4},{6,5},{7,6},{8,15},{9,8},{10,9... | collective-permute-start | bytes 1327112 | tf_op jit(solution)/shard_map/ppermute | solution.py:17
  20.8 3.2 %collective-permute-start.6 = (bf16[2,32,128]{2,1,0:T(8,128)(2,1)S(1)}, bf16[2,32,128]{2,1,0:T(8,128)(2,1)S(1)}, u32[]{:S(2)}, u32[]{:S(2)}) collective-permute-start(bf16[2,32,128]{2,1,0:T(8,128)(2,1)S(1)} %get-tuple-element.39), channel_id=1, source_target_pairs={{0,1},{1,2},{2,3},{3,4},{4,5},{5,6},{6,7},{7,0},{8,9},{9,10},{10,1... | collective-permute-start | bytes 49160 | tf_op jit(solution)/shard_map/ppermute | solution.py:17
  24.0 4.6 %collective-permute-start.7 = (bf16[2,32,128]{2,1,0:T(8,128)(2,1)S(1)}, bf16[2,32,128]{2,1,0:T(8,128)(2,1)S(1)}, u32[]{:S(2)}, u32[]{:S(2)}) collective-permute-start(bf16[2,32,128]{2,1,0:T(8,128)(2,1)S(1)} %get-tuple-element.40), channel_id=1, source_target_pairs={{0,7},{1,0},{2,1},{3,2},{4,3},{5,4},{6,5},{7,6},{8,15},{9,8},{10,9... | collective-permute-start | bytes 49160 | tf_op jit(solution)/shard_map/ppermute | solution.py:17
  29.4 43.6 %copy-start.12 = (bf16[3,1,32,3,192]{4,2,3,0,1:T(8,128)(2,1)S(1)}, bf16[3,1,32,3,192]{4,2,3,0,1:T(8,128)(2,1)}, u32[]{:S(2)}) copy-start(bf16[3,1,32,3,192]{4,2,3,0,1:T(8,128)(2,1)} %get-tuple-element.33) | copy-start | bytes 331780
  29.4 43.6 %copy-start.13 = (bf16[3,1,32,3,192]{4,2,3,0,1:T(8,128)(2,1)S(1)}, bf16[3,1,32,3,192]{4,2,3,0,1:T(8,128)(2,1)}, u32[]{:S(2)}) copy-start(bf16[3,1,32,3,192]{4,2,3,0,1:T(8,128)(2,1)} %get-tuple-element.34) | copy-start | bytes 331780
  41.7 43.8 %collective-permute-start.11 = (bf16[56,32,128]{2,1,0:T(8,128)(2,1)}, bf16[56,32,128]{2,1,0:T(8,128)(2,1)S(1)}, u32[]{:S(2)}, u32[]{:S(2)}) collective-permute-start(bf16[56,32,128]{2,1,0:T(8,128)(2,1)} %get-tuple-element.11.after), channel_id=1, source_target_pairs={{0,7},{1,0},{2,1},{3,2},{4,3},{5,4},{6,5},{7,6},{8,15},{9,8},{10,9... | collective-permute-start | bytes 1376264 | tf_op jit(solution)/shard_map/ppermute | solution.py:17
  58.9 14.2 %copy-start.7 = (bf16[56,32,128]{2,1,0:T(8,128)(2,1)}, bf16[56,32,128]{2,1,0:T(8,128)(2,1)S(1)}, u32[]{:S(2)}) copy-start(bf16[56,32,128]{2,1,0:T(8,128)(2,1)S(1)} %get-tuple-element.13) | copy-start | bytes 1376260
  60.3 25.3 %collective-permute-start.10 = (bf16[56,32,128]{2,1,0:T(8,128)(2,1)}, bf16[56,32,128]{2,1,0:T(8,128)(2,1)S(1)}, u32[]{:S(2)}, u32[]{:S(2)}) collective-permute-start(bf16[56,32,128]{2,1,0:T(8,128)(2,1)} %get-tuple-element.16), channel_id=1, source_target_pairs={{0,1},{1,2},{2,3},{3,4},{4,5},{5,6},{6,7},{7,0},{8,9},{9,10},{10,1... | collective-permute-start | bytes 1376264 | tf_op jit(solution)/shard_map/ppermute | solution.py:17
  60.3 16.1 %collective-permute-start.12 = (bf16[32,128]{1,0:T(8,128)(2,1)}, bf16[32,128]{1,0:T(8,128)(2,1)S(1)}, u32[]{:S(2)}, u32[]{:S(2)}) collective-permute-start(bf16[32,128]{1,0:T(8,128)(2,1)} %get-tuple-element.25), channel_id=1, source_target_pairs={{0,9},{1,10},{2,11},{3,12},{4,13},{5,14},{6,15},{7,8},{8,17},{9,18... | collective-permute-start | bytes 24584 | tf_op jit(solution)/shard_map/ppermute | solution.py:38
  64.9 12.8 %collective-permute-start.14 = (bf16[32,128]{1,0:T(8,128)(2,1)}, bf16[32,128]{1,0:T(8,128)(2,1)S(1)}, u32[]{:S(2)}, u32[]{:S(2)}) collective-permute-start(bf16[32,128]{1,0:T(8,128)(2,1)} %get-tuple-element.28), channel_id=1, source_target_pairs={{0,15},{1,8},{2,9},{3,10},{4,11},{5,12},{6,13},{7,14},{8,23},{9,16... | collective-permute-start | bytes 24584 | tf_op jit(solution)/shard_map/ppermute | solution.py:38
  68.9 10.1 %collective-permute-start.13 = (bf16[4,32,128]{2,1,0:T(8,128)(2,1)}, bf16[4,32,128]{2,1,0:T(8,128)(2,1)}, u32[]{:S(2)}, u32[]{:S(2)}) collective-permute-start(bf16[4,32,128]{2,1,0:T(8,128)(2,1)} %get-tuple-element.29), channel_id=1, source_target_pairs={{0,8},{8,16},{16,24},{1,9},{9,17},{17,25},{2,10},{10,18},{18,26},{... | collective-permute-start | bytes 98312 | tf_op jit(solution)/shard_map/ppermute | solution.py:17
  76.4 5.9 %collective-permute-start.15 = (bf16[32,128]{1,0:T(8,128)(2,1)S(1)}, bf16[32,128]{1,0:T(8,128)(2,1)S(1)}, u32[]{:S(2)}, u32[]{:S(2)}) collective-permute-start(bf16[32,128]{1,0:T(8,128)(2,1)S(1)} %copy-done.20), channel_id=1, source_target_pairs={{8,1},{9,2},{10,3},{11,4},{12,5},{13,6},{14,7},{15,0},{16,9},{17,1... | collective-permute-start | bytes 24584 | tf_op jit(solution)/shard_map/ppermute | solution.py:38
  77.7 6.6 %collective-permute-start.17 = (bf16[32,128]{1,0:T(8,128)(2,1)S(1)}, bf16[32,128]{1,0:T(8,128)(2,1)S(1)}, u32[]{:S(2)}, u32[]{:S(2)}) collective-permute-start(bf16[32,128]{1,0:T(8,128)(2,1)S(1)} %get-tuple-element.26), channel_id=1, source_target_pairs={{8,7},{9,0},{10,1},{11,2},{12,3},{13,4},{14,5},{15,6},{16,15},{17,... | collective-permute-start | bytes 24584 | tf_op jit(solution)/shard_map/ppermute | solution.py:38
  79.1 6.4 %collective-permute-start.16 = (bf16[4,32,128]{2,1,0:T(8,128)(2,1)S(1)}, bf16[4,32,128]{2,1,0:T(8,128)(2,1)S(1)}, u32[]{:S(2)}, u32[]{:S(2)}) collective-permute-start(bf16[4,32,128]{2,1,0:T(8,128)(2,1)S(1)} %copy-done.19), channel_id=1, source_target_pairs={{8,0},{16,8},{24,16},{9,1},{17,9},{25,17},{10,2},{18,10},{26,18},{... | collective-permute-start | bytes 98312 | tf_op jit(solution)/shard_map/ppermute | solution.py:17
  82.3 13.4 %collective-permute-start.9 = (bf16[56,32,128]{2,1,0:T(8,128)(2,1)}, bf16[56,32,128]{2,1,0:T(8,128)(2,1)S(1)}, u32[]{:S(2)}, u32[]{:S(2)}) collective-permute-start(bf16[56,32,128]{2,1,0:T(8,128)(2,1)} %copy-done.8), channel_id=1, source_target_pairs={{0,7},{1,0},{2,1},{3,2},{4,3},{5,4},{6,5},{7,6},{8,15},{9,8},{10,9... | collective-permute-start | bytes 1376264 | tf_op jit(solution)/shard_map/ppermute | solution.py:17
  84.3 11.8 %collective-permute-start.8 = (bf16[56,32,128]{2,1,0:T(8,128)(2,1)}, bf16[56,32,128]{2,1,0:T(8,128)(2,1)S(1)}, u32[]{:S(2)}, u32[]{:S(2)}) collective-permute-start(bf16[56,32,128]{2,1,0:T(8,128)(2,1)} %copy-done.7), channel_id=1, source_target_pairs={{0,1},{1,2},{2,3},{3,4},{4,5},{5,6},{6,7},{7,0},{8,9},{9,10},{10,1... | collective-permute-start | bytes 1376264 | tf_op jit(solution)/shard_map/ppermute | solution.py:17
  111.1 29.5 %all-to-all-start.1 = ((bf16[8,32,32,128]{3,2,1,0:T(8,128)(2,1)}), bf16[8,32,32,128]{3,2,1,0:T(8,128)(2,1)S(1)}, u32[]{:S(2)}, u32[]{:S(2)}) async-start(bf16[8,32,32,128]{3,2,1,0:T(8,128)(2,1)} %bitcast.93), calls=%async_computation.1 | async-start | bytes 4194304 | tf_op jit(solution)/shard_map/all_to_all | solution.py:332
  (19 other events, 106.6 us)

commit v2 on v0

v2 whole, which is shorter than its diff:
```python
import functools

import jax
import jax.numpy as jnp
from jax import lax
from jax.experimental import pallas as pl
from jax.experimental.pallas import tpu as pltpu
from jax.sharding import PartitionSpec as P

CB_DEV = 12
VMEM_LIMIT = 48 * 1024 * 1024


def mixing(weight, phi_len):
    channels = weight.shape[3]
    base = jnp.transpose(weight[::-1, ::-1], (2, 3, 0, 1, 4))
    base = base.reshape(3, channels, 3, 3 * channels)
    rows = [
        jnp.pad(base, ((0, 0), (0, 0), (0, 0), (p * channels, (phi_len - 1 - p) * channels)))
        for p in range(phi_len)
    ]
    full = jnp.stack(rows, axis=1)
    return full.reshape(3 * phi_len * channels, 3 * (phi_len + 2) * channels)


def conv_pair(xp, w_ref, z):
    slabs = [xp[z + k].reshape(192, 128) for k in range(4)]
    rhs = jnp.concatenate(
        [jnp.concatenate([slabs[k], slabs[k + 1]], axis=1) for k in range(3)], axis=0
    )
    y = jnp.dot(w_ref[...], rhs, preferred_element_type=jnp.float32)
    lane = lax.broadcasted_iota(jnp.int32, (128, 128), 1)
    outs = []
    for k in range(2):
        cols = slice(128 * k, 128 * k + 128)
        minus = pltpu.roll(y[0:128, cols], 127, 1)
        plus = pltpu.roll(y[256:384, cols], 1, 1)
        outs.append(
            y[128:256, cols]
            + jnp.where(lane == 127, 0.0, minus)
            + jnp.where(lane == 0, 0.0, plus)
        )
    return outs


def convolve(xp, w_ref, first, cells, store):
    def step(t, carry):
        z = first + t * 2
        for k, back in enumerate(conv_pair(xp, w_ref, z)):
            store(back, z + k)
        return carry

    lax.fori_loop(0, cells // 2, step, 0, unroll=4)


def grid_kernel(
    depths, phis, x_ref, pre_ref, w2_ref, w1_ref, out_ref, xp, hp, pre, send, recv, local
):
    depth = x_ref.shape[0]
    d = lax.axis_index("depth")
    p = lax.axis_index("phi")
    right = lax.rem(p + 1, phis)
    left = lax.rem(p + phis - 1, phis)
    inner = depth // 4 - 4
    core = depth // 4 + 4
    has_below = d > 0
    has_above = d < depths - 1
    mesh_ids = pl.DeviceIdType.MESH

    fill = pltpu.make_async_copy(x_ref, xp.at[pl.ds(1, depth), pl.ds(1, 4)], local.at[0])
    fill.start()
    load = pltpu.make_async_copy(pre_ref, pre, local.at[1])
    load.start()

    barrier = pltpu.get_barrier_semaphore()
    for q in (left, right):
        pl.semaphore_signal(barrier, inc=1, device_id=(d, q), device_id_type=mesh_ids)
    for exists, step in ((has_below, -1), (has_above, 1)):

        @pl.when(exists)
        def _(step=step):
            for q in (left, p, right):
                pl.semaphore_signal(barrier, inc=1, device_id=(d + step, q), device_id_type=mesh_ids)

    peers = 2 + 3 * has_below.astype(jnp.int32) + 3 * has_above.astype(jnp.int32)
    pl.semaphore_wait(barrier, peers)

    def remote(src, dst, stage, index, to):
        return pltpu.make_async_remote_copy(
            src_ref=src,
            dst_ref=dst,
            send_sem=send.at[stage, index],
            recv_sem=recv.at[stage, index],
            device_id=to,
            device_id_type=mesh_ids,
        )

    def faces(src, z_at, phi_at, dst, stage, index, first, cells):
        zs = pl.ds(first + z_at, cells)
        to = pl.ds(first + 1, cells)
        return [
            remote(src.at[zs, phi_at + 3], dst.at[to, 0], stage, index, (d, right)),
            remote(src.at[zs, phi_at], dst.at[to, 5], stage, index + 1, (d, left)),
        ]

    def layers(src, z_at, phi_at, dst, stage, step):
        z = z_at + (depth - 1 if step > 0 else 0)
        to = 0 if step > 0 else depth + 1
        index = 6 if step > 0 else 9
        mine = src.at[z]
        return [
            remote(mine.at[pl.ds(phi_at, 4)], dst.at[to, pl.ds(1, 4)], stage, index, (d + step, p)),
            remote(mine.at[phi_at + 3], dst.at[to, 0], stage, index + 1, (d + step, right)),
            remote(mine.at[phi_at], dst.at[to, 5], stage, index + 2, (d + step, left)),
        ]

    def sends(src, z_at, phi_at, dst, stage, cut):
        mid = faces(src, z_at, phi_at, dst, stage, 0, cut, depth - 2 * cut)
        outer = faces(src, z_at, phi_at, dst, stage, 2, 0, cut)
        outer += faces(src, z_at, phi_at, dst, stage, 4, depth - cut, cut)
        up = layers(src, z_at, phi_at, dst, stage, 1)
        down = layers(src, z_at, phi_at, dst, stage, -1)
        return mid, outer, up, down

    def start_outer(outer, up, down):
        for exists, group in ((has_above, up), (has_below, down)):

            @pl.when(exists)
            def _(group=group):
                for c in group:
                    c.start()

        for c in outer:
            c.start()

    def wait_outer(outer, up, down):
        for c in outer:
            c.wait_recv()
        for exists, group in ((has_below, up), (has_above, down)):

            @pl.when(exists)
            def _(group=group):
                for c in group:
                    c.wait_recv()

    first = sends(x_ref, 0, 0, xp, 0, inner - 1)
    second = sends(hp, 1, 1, hp, 1, inner)
    for c in first[0]:
        c.start()
    start_outer(*first[1:])

    zeros = jnp.zeros((6, 32, 128), jnp.bfloat16)
    for buf in (xp, hp):

        @pl.when(d == 0)
        def _(buf=buf):
            buf[0] = zeros

        @pl.when(d == depths - 1)
        def _(buf=buf):
            buf[depth + 1] = zeros

    def store_hidden(back, z):
        v = pre[z].reshape(128, 128).astype(jnp.float32)
        s = 1.0 / (1.0 + jnp.exp(-v))
        hid = (back * s * (1.0 + v * (1.0 - s))).astype(jnp.bfloat16)
        hp[z + 1, 1:5] = hid.reshape(4, 32, 128)

    def store_grid(back, z):
        g = xp[z + 1, 1:5].reshape(128, 128).astype(jnp.float32)
        out_ref[z] = (back + g).astype(jnp.bfloat16).reshape(4, 32, 128)

    fill.wait()
    load.wait()
    for c in first[0]:
        c.wait_recv()
    convolve(xp, w2_ref, inner, depth - 2 * inner, store_hidden)
    for c in second[0]:
        c.start()
    wait_outer(*first[1:])
    convolve(xp, w2_ref, 0, inner, store_hidden)
    convolve(xp, w2_ref, depth - inner, inner, store_hidden)
    start_outer(*second[1:])
    for c in second[0]:
        c.wait_recv()
    convolve(hp, w1_ref, core, depth - 2 * core, store_grid)
    wait_outer(*second[1:])
    convolve(hp, w1_ref, 0, core, store_grid)
    convolve(hp, w1_ref, depth - core, core, store_grid)
    for mid, outer, up, down in (first, second):
        for c in mid + outer:
            c.wait_send()
        for exists, group in ((has_above, up), (has_below, down)):

            @pl.when(exists)
            def _(group=group):
                for c in group:
                    c.wait_send()


def map_kernel(row_ref, pos_ref, grid, map_ref, buf_ref):
    def clear(t, carry):
        buf_ref[pl.ds(t * 8, 8)] = jnp.zeros((8, 32, 128), jnp.bfloat16)
        return carry

    lax.fori_loop(0, buf_ref.shape[0] // 8, clear, 0)

    def block(t, carry):
        for k in range(16):
            n = t * 16 + k
            part = jnp.dot(grid[row_ref[n]], map_ref[n], preferred_element_type=jnp.float32)
            buf_ref[pos_ref[n]] = part.astype(jnp.bfloat16)
        return carry

    lax.fori_loop(0, map_ref.shape[0] // 16, block, 0)


def gather_kernel(target_ref, recv_ref, out_ref, acc):
    acc[...] = jnp.zeros_like(acc)

    def step(t, carry):
        for k in range(4):
            n = t * 4 + k
            c = target_ref[n]
            acc[c] = acc[c] + recv_ref[n].astype(jnp.float32)
        return carry

    lax.fori_loop(0, recv_ref.shape[0] // 4, step, 0)
    out_ref[...] = acc[0 : out_ref.shape[0]].astype(jnp.bfloat16)


def vmem():
    return pl.BlockSpec(memory_space=pltpu.VMEM)


def smem():
    return pl.BlockSpec(memory_space=pltpu.SMEM)


def body(grad_out, pre_act, w_first, w_second, map_blocks, row_block, owner, col_local):
    depth, phi_len, channels, eta = grad_out.shape
    rows = depth * phi_len
    bf16 = jnp.bfloat16
    depth_count = lax.axis_size("depth")
    phi_count = lax.axis_size("phi")
    owners = depth_count * phi_count
    block_count = map_blocks.shape[0]
    cell_size = map_blocks.shape[2]
    slots = max(2, 2 * block_count // owners)
    places = owners * slots
    padded = (depth + 2, phi_len + 2, channels, eta)

    owner_ids = owner[:, 0]
    count = jnp.arange(block_count, dtype=jnp.int32)
    same = (owner_ids[:, None] == owner_ids[None, :]) & (count[None, :] < count[:, None])
    slot_index = jnp.sum(same.astype(jnp.int32), axis=1)
    owner_depth = owner_ids // phi_count
    owner_phi = owner_ids - owner_depth * phi_count
    position = (owner_phi * depth_count + owner_depth) * slots + slot_index
    taken = position[:, None] == jnp.arange(places, dtype=jnp.int32)[None, :]
    slot_cells = jnp.sum(
        jnp.where(taken, col_local.astype(jnp.float32)[:, None] + 1.0, 0.0), axis=0
    )
    got_cells = lax.all_to_all(
        slot_cells.reshape(phi_count, depth_count * slots), "phi", 0, 0, tiled=True
    )
    cells = got_cells.reshape(phi_count, depth_count, slots).astype(jnp.int32)
    base = (jnp.arange(depth_count, dtype=jnp.int32) * CB_DEV)[None, :, None]
    target = jnp.where(cells > 0, base + cells - 1, depth_count * CB_DEV).reshape(places)

    mix_second = mixing(w_second, phi_len)
    mix_first = mixing(w_first, phi_len)
    grid = pl.pallas_call(
        functools.partial(grid_kernel, depth_count, phi_count),
        out_shape=jax.ShapeDtypeStruct(grad_out.shape, bf16),
        in_specs=[pl.BlockSpec(memory_space=pl.ANY)] * 2 + [vmem()] * 2,
        out_specs=vmem(),
        scratch_shapes=[
            pltpu.VMEM(padded, bf16),
            pltpu.VMEM(padded, bf16),
            pltpu.VMEM(pre_act.shape[:1] + (phi_len, channels, eta), bf16),
            pltpu.SemaphoreType.DMA((2, 12)),
            pltpu.SemaphoreType.DMA((2, 12)),
            pltpu.SemaphoreType.DMA((2,)),
        ],
        compiler_params=pltpu.CompilerParams(
            vmem_limit_bytes=VMEM_LIMIT, collective_id=0, has_side_effects=True
        ),
    )(grad_out, pre_act, mix_second, mix_first)
    buffer = pl.pallas_call(
        map_kernel,
        out_shape=jax.ShapeDtypeStruct((places, channels, cell_size), bf16),
        in_specs=[smem()] * 2 + [vmem()] * 2,
        out_specs=vmem(),
        compiler_params=pltpu.CompilerParams(vmem_limit_bytes=VMEM_LIMIT),
    )(row_block, position, grid.reshape(rows, channels, eta), map_blocks)

    received = lax.all_to_all(
        buffer.reshape(phi_count, depth_count * slots, channels, cell_size), "phi", 0, 0, tiled=True
    ).reshape(places, channels, cell_size)
    sums = pl.pallas_call(
        gather_kernel,
        out_shape=jax.ShapeDtypeStruct((depth_count * CB_DEV, channels, cell_size), bf16),
        in_specs=[smem(), vmem()],
        out_specs=vmem(),
        scratch_shapes=[pltpu.VMEM((depth_count * CB_DEV + 1, channels, cell_size), jnp.float32)],
        compiler_params=pltpu.CompilerParams(vmem_limit_bytes=VMEM_LIMIT),
    )(target, received)
    parts = lax.all_to_all(
        sums.reshape(depth_count, CB_DEV, channels, cell_size), "depth", 0, 0, tiled=True
    )
    return jnp.sum(parts.astype(jnp.float32), axis=0)


def solution(mesh):
    return jax.shard_map(
        body,
        mesh=mesh,
        in_specs=(
            P("depth", "phi", None, None),
            P("depth", "phi", None, None),
            P(),
            P(),
            P(("depth", "phi"), None, None),
            P(("depth", "phi")),
            P(("depth", "phi"), None),
            P(("depth", "phi")),
        ),
        out_specs=P(("depth", "phi"), None, None),
        check_vma=False,
    )
```

time: 167 us -> 122 us (0.73)
  waiting for transfers between devices: 44.6 us -> 24.9 us
  starting transfers between devices: 28 us -> 10.9 us
  local copies, waits for them, and re-layouts: 11 us -> 6.08 us
  Pallas kernels: 63.5 us -> 59.5 us
  other arithmetic: 1.37 us -> 4.05 us
  blocking collectives: 17.8 us -> 15.8 us
    ppermute x12 -> x0, waiting for transfers between devices: 19.8 us -> none  [shift(): return lax.ppermute(block, axis, pairs)]
    ppermute x12 -> x0, starting transfers between devices: 17.9 us -> none  [shift(): return lax.ppermute(block, axis, pairs)]
    pallas_call x2, Pallas kernels: 61.6 us -> 57.5 us  [the longest x1 51.6 us: body(): pl.pallas_call(functools.partial(grid_kernel, depth_count, phi_count), ou...]
    squeeze x2 -> x0, local copies, waits for them, and re-layouts: 3.9 us -> none  [the longest x1 3.06 us: body(): high = shift(grad_out[:, 0], 'phi', -1, True)]
    all_to_all x1, blocking collectives: 17.8 us -> 15.8 us  [body(): lax.all_to_all(sums.reshape(depth_count, CB_DEV, channels, cell_size), 'd...]
    transpose x4, local copies, waits for them, and re-layouts: 0.34 us -> 2.21 us  [mixing(): base = jnp.transpose(weight[::-1, ::-1], (2, 3, 0, 1, 4))]
  transfers between devices with their start and end apart: 14 -> 2, of which waited for: 7 -> 1; matrix products, arithmetic and copies ran while one was open for 6% -> 5% of each run, Pallas kernels for 37% -> 47%
where the time goes in v2:
time: 122 us; the launch traced here: 121 us
  Pallas kernels  59.5 us (49%)
  waiting for transfers between devices  24.9 us (20%)
  blocking collectives  15.8 us (13%)
  starting transfers between devices  10.9 us (9%)
  local copies, waits for them, and re-layouts  6.08 us (5%)
  other arithmetic  4.05 us (3%)
    pallas_call x1, Pallas kernels, body(): pl.pallas_call(functools.partial(grid_kernel, depth_count, phi_count), ou...  51.6 us
    all_to_all x1, waiting for transfers between devices, body(): lax.all_to_all(buffer.reshape(phi_count, depth_count * slots, channels, c...  24.9 us
    all_to_all x1, blocking collectives, body(): lax.all_to_all(sums.reshape(depth_count, CB_DEV, channels, cell_size), 'd...  15.8 us
    all_to_all x1, starting transfers between devices, body(): lax.all_to_all(buffer.reshape(phi_count, depth_count * slots, channels, c...  6.63 us
    pallas_call x1, Pallas kernels, body(): pl.pallas_call(map_kernel, out_shape=jax.ShapeDtypeStruct((places, channe...  5.91 us
    all_to_all x1, starting transfers between devices, body(): lax.all_to_all(slot_cells.reshape(phi_count, depth_count * slots), 'phi',...  4.25 us
  transfers between devices with their start and end apart: 2, of which 1 were waited for; matrix products, arithmetic and copies ran while one was open for 5% of the time, Pallas kernels for 47%

profile of v2, /device:TPU:2, one launch (start us, length us, event | category | flops | bytes accessed | tf_op | source)
XLA Modules:
  0.0 121.4 jit_solution(14946260571062125259)
XLA Ops:
  0.0 0.9 convert_reduce_fusion.1
  0.9 0.7 fusion.1
  1.6 0.7 convert_add_fusion
  2.4 0.7 all_to_all.12
  3.0 4.3 %all-to-all-start = ((f32[8,1,32]{2,1,0:T(1,128)}), f32[8,1,32]{2,1,0:T(1,128)S(1)}, u32[]{:S(2)}, u32[]{:S(2)}) async-start(f32[8,1,32]{2,1,0:T(1,128)} %all_to_all.12), calls=%async_computation | async-start | bytes 8192 | tf_op jit(solution)/shard_map/all_to_all | solution.py:264
  7.3 0.7 multiply_add_fusion.pos_ref
  8.0 1.0 reverse_bitcast_fusion
  8.9 0.2 copy.21
  9.1 0.2 reshape.44
  9.2 0.2 pad_bitcast_fusion.3
  9.5 1.0 reverse_bitcast_fusion.1
  10.6 0.2 reshape.42
  10.7 0.2 pad_bitcast_fusion.7
  11.2 0.5 copy.22
  11.8 0.6 reshape.45.w1_ref
  12.4 0.5 copy.20
  12.9 0.6 reshape.43.w2_ref
  13.5 51.6 %shard_map.82 = bf16[112,4,32,128]{3,2,1,0:T(8,128)(2,1)S(1)} custom-call(bf16[112,4,32,128]{3,2,1,0:T(8,128)(2,1)} %x_ref.1, bf16[112,4,32,128]{3,2,1,0:T(8,128)(2,1)} %pre_ref.1, bf16[384,576]{1,0:T(8,128)(2,1)S(1)} %reshape.43.w2_ref, bf16[384,576]{1,0:T(8,128)(2,1)S(1)} %reshape.45.w1_ref), custom_call_target="tpu_custom_call" | custom-call | tf_op jit(solution)/shard_map/pallas_call | solution.py:273
  65.1 5.9 %shard_map.83 = bf16[256,32,128]{2,1,0:T(8,128)(2,1)} custom-call(s32[128]{0:T(128)S(1)} %copy-done, s32[128]{0:T(128)S(1)} %multiply_add_fusion.pos_ref, bf16[448,32,128]{2,1,0:T(8,128)(2,1)S(1)} %bitcast.36, bf16[128,128,128]{2,1,0:T(8,128)(2,1)} %map_ref.1), custom_call_target="tpu_custom_call" | custom-call | tf_op jit(solution)/shard_map/pallas_call | solution.py:290
  71.1 6.6 %all-to-all-start.1 = ((bf16[8,32,32,128]{3,2,1,0:T(8,128)(2,1)}), bf16[8,32,32,128]{3,2,1,0:T(8,128)(2,1)S(1)}, u32[]{:S(2)}, u32[]{:S(2)}) async-start(bf16[8,32,32,128]{3,2,1,0:T(8,128)(2,1)} %bitcast.14), calls=%async_computation.1 | async-start | bytes 4194304 | tf_op jit(solution)/shard_map/all_to_all | solution.py:298
  78.0 24.9 %all-to-all-done.1 = bf16[8,32,32,128]{3,2,1,0:T(8,128)(2,1)S(1)} async-done(((bf16[8,32,32,128]{3,2,1,0:T(8,128)(2,1)}), bf16[8,32,32,128]{3,2,1,0:T(8,128)(2,1)S(1)}, u32[]{:S(2)}, u32[]{:S(2)}) %all-to-all-start.1) | async-done | bytes 2097184 | tf_op jit(solution)/shard_map/all_to_all | solution.py:298
  102.8 2.0 %shard_map.84 = bf16[48,32,128]{2,1,0:T(8,128)(2,1)S(1)} custom-call(s32[256]{0:T(256)S(1)} %compare_select_fusion.target_ref, bf16[256,32,128]{2,1,0:T(8,128)(2,1)S(1)} %bitcast.37), custom_call_target="tpu_custom_call" | custom-call | tf_op jit(solution)/shard_map/pallas_call | solution.py:301
  104.8 15.8 %all_to_all.19 = bf16[4,12,32,128]{3,2,1,0:T(8,128)(2,1)S(1)} all-to-all(bf16[4,12,32,128]{3,2,1,0:T(8,128)(2,1)S(1)} %bitcast.38), channel_id=1, replica_groups=mesh['depth'=4,'phi'=8] {'depth'}, dimensions={0} | all-to-all | bytes 786432 | tf_op jit(solution)/shard_map/all_to_all | solution.py:309
  120.6 0.7 convert_reduce_fusion
  (13 shorter events, 0.8 us)
Async XLA Ops:
  3.0 68.0 %all-to-all-start = ((f32[8,1,32]{2,1,0:T(1,128)}), f32[8,1,32]{2,1,0:T(1,128)S(1)}, u32[]{:S(2)}, u32[]{:S(2)}) async-start(f32[8,1,32]{2,1,0:T(1,128)} %all_to_all.12), calls=%async_computation | async-start | bytes 8192 | tf_op jit(solution)/shard_map/all_to_all | solution.py:264
  13.5 51.7 %copy-start = (s32[128]{0:T(128)S(1)}, s32[128]{0:T(128)}, u32[]{:S(2)}) copy-start(s32[128]{0:T(128)} %row_ref.1) | copy-start | bytes 1540
  71.1 31.8 %all-to-all-start.1 = ((bf16[8,32,32,128]{3,2,1,0:T(8,128)(2,1)}), bf16[8,32,32,128]{3,2,1,0:T(8,128)(2,1)S(1)}, u32[]{:S(2)}, u32[]{:S(2)}) async-start(bf16[8,32,32,128]{3,2,1,0:T(8,128)(2,1)} %bitcast.14), calls=%async_computation.1 | async-start | bytes 4194304 | tf_op jit(solution)/shard_map/all_to_all | solution.py:298

commit v3 on v2

--- a/solution.py
+++ b/solution.py
@@ -227,6 +227,53 @@
 
     lax.fori_loop(0, recv_ref.shape[0] // 4, step, 0)
     out_ref[...] = acc[0 : out_ref.shape[0]].astype(jnp.bfloat16)
+
+
+def exchange_kernel(axis, count, x_ref, out_ref, send, recv, local):
+    me = lax.axis_index(axis)
+    barrier = pltpu.get_barrier_semaphore()
+    peers = [lax.rem(me + k, count) for k in range(1, count)]
+    for peer in peers:
+        pl.semaphore_signal(
+            barrier, inc=1, device_id={axis: peer}, device_id_type=pl.DeviceIdType.MESH
+        )
+    own = pltpu.make_async_copy(x_ref.at[me], out_ref.at[me], local)
+    own.start()
+    pl.semaphore_wait(barrier, count - 1)
+    copies = [
+        pltpu.make_async_remote_copy(
+            src_ref=x_ref.at[peer],
+            dst_ref=out_ref.at[me],
+            send_sem=send.at[k],
+            recv_sem=recv.at[k],
+            device_id={axis: peer},
+            device_id_type=pl.DeviceIdType.MESH,
+        )
+        for k, peer in enumerate(peers)
+    ]
+    for c in copies:
+        c.start()
+    own.wait()
+    for c in copies:
+        c.wait()
+
+
+def exchange(x, axis, collective):
+    count = lax.axis_size(axis)
+    return pl.pallas_call(
+        functools.partial(exchange_kernel, axis, count),
+        out_shape=jax.ShapeDtypeStruct(x.shape, x.dtype),
+        in_specs=[vmem()],
+        out_specs=vmem(),
+        scratch_shapes=[
+            pltpu.SemaphoreType.DMA((count - 1,)),
+            pltpu.SemaphoreType.DMA((count - 1,)),
+            pltpu.SemaphoreType.DMA,
+        ],
+        compiler_params=pltpu.CompilerParams(
+            vmem_limit_bytes=VMEM_LIMIT, collective_id=collective, has_side_effects=True
+        ),
+    )(x)
 
 
 def vmem():
@@ -295,8 +342,8 @@
         compiler_params=pltpu.CompilerParams(vmem_limit_bytes=VMEM_LIMIT),
     )(row_block, position, grid.reshape(rows, channels, eta), map_blocks)
 
-    received = lax.all_to_all(
-        buffer.reshape(phi_count, depth_count * slots, channels, cell_size), "phi", 0, 0, tiled=True
+    received = exchange(
+        buffer.reshape(phi_count, depth_count * slots, channels, cell_size), "phi", 1
     ).reshape(places, channels, cell_size)
     sums = pl.pallas_call(
         gather_kernel,
@@ -306,9 +353,7 @@
         scratch_shapes=[pltpu.VMEM((depth_count * CB_DEV + 1, channels, cell_size), jnp.float32)],
         compiler_params=pltpu.CompilerParams(vmem_limit_bytes=VMEM_LIMIT),
     )(target, received)
-    parts = lax.all_to_all(
-        sums.reshape(depth_count, CB_DEV, channels, cell_size), "depth", 0, 0, tiled=True
-    )
+    parts = exchange(sums.reshape(depth_count, CB_DEV, channels, cell_size), "depth", 2)
     return jnp.sum(parts.astype(jnp.float32), axis=0)
 
 

time: 122 us -> 112 us (0.918)
  the two profiles are of different devices: /device:TPU:2 before, /device:TPU:1 now
where the time goes in v3:
time: 112 us
  Pallas kernels  96.4 us (86%)
  local copies, waits for them, and re-layouts  6.08 us (5%)
  starting transfers between devices  5.22 us (5%)
  other arithmetic  4.05 us (4%)
    pallas_call x1, Pallas kernels, body(): pl.pallas_call(functools.partial(grid_kernel, depth_count, phi_count), ou...  50.8 us
    pallas_call x2, Pallas kernels, exchange(): pl.pallas_call(functools.partial(exchange_kernel, axis, count), out_shape...  39.1 us
    all_to_all x1, starting transfers between devices, body(): lax.all_to_all(slot_cells.reshape(phi_count, depth_count * slots), 'phi',...  5.22 us
    pallas_call x1, Pallas kernels, body(): pl.pallas_call(map_kernel, out_shape=jax.ShapeDtypeStruct((places, channe...  4.55 us
  transfers between devices with their start and end apart: 1, of which 0 were waited for; matrix products, arithmetic and copies ran while one was open for 6% of the time, Pallas kernels for 75%

profile of v3, /device:TPU:1, one launch (start us, length us, event | category | flops | bytes accessed | tf_op | source)
XLA Modules:
  0.0 111.9 jit_solution(4898012985355003540)
XLA Ops:
  0.0 0.9 convert_reduce_fusion.1
  0.9 0.7 fusion.1
  1.6 0.7 convert_add_fusion
  2.4 0.7 all_to_all.6
  3.0 5.2 %all-to-all-start = ((f32[8,1,32]{2,1,0:T(1,128)}), f32[8,1,32]{2,1,0:T(1,128)S(1)}, u32[]{:S(2)}, u32[]{:S(2)}) async-start(f32[8,1,32]{2,1,0:T(1,128)} %all_to_all.6), calls=%async_computation | async-start | bytes 8192 | tf_op jit(solution)/shard_map/all_to_all | solution.py:311
  8.3 0.7 multiply_add_fusion.pos_ref
  8.9 1.0 reverse_bitcast_fusion
  9.9 0.2 copy.21
  10.0 0.2 reshape.44
  10.2 0.2 pad_bitcast_fusion.3
  10.4 1.0 reverse_bitcast_fusion.1
  11.4 0.2 copy.19
  11.5 0.2 reshape.42
  11.7 0.2 pad_bitcast_fusion.7
  12.2 0.5 copy.22
  12.7 0.6 reshape.45.w1_ref
  13.3 0.5 copy.20
  13.9 0.6 reshape.43.w2_ref
  14.5 50.8 %shard_map.82 = bf16[112,4,32,128]{3,2,1,0:T(8,128)(2,1)S(1)} custom-call(bf16[112,4,32,128]{3,2,1,0:T(8,128)(2,1)} %x_ref.1, bf16[112,4,32,128]{3,2,1,0:T(8,128)(2,1)} %pre_ref.1, bf16[384,576]{1,0:T(8,128)(2,1)S(1)} %reshape.43.w2_ref, bf16[384,576]{1,0:T(8,128)(2,1)S(1)} %reshape.45.w1_ref), custom_call_target="tpu_custom_call" | custom-call | tf_op jit(solution)/shard_map/pallas_call | solution.py:320
  65.3 4.5 %shard_map.83 = bf16[256,32,128]{2,1,0:T(8,128)(2,1)S(1)} custom-call(s32[128]{0:T(128)S(1)} %copy-done, s32[128]{0:T(128)S(1)} %multiply_add_fusion.pos_ref, bf16[448,32,128]{2,1,0:T(8,128)(2,1)S(1)} %bitcast.36, bf16[128,128,128]{2,1,0:T(8,128)(2,1)} %map_ref.1), custom_call_target="tpu_custom_call" | custom-call | tf_op jit(solution)/shard_map/pallas_call | solution.py:337
  69.9 29.0 %shard_map.84 = bf16[8,32,32,128]{3,2,1,0:T(8,128)(2,1)S(1)} custom-call(bf16[8,32,32,128]{3,2,1,0:T(8,128)(2,1)S(1)} %bitcast.37), custom_call_target="tpu_custom_call" | custom-call | tf_op jit(solution)/shard_map/pallas_call | solution.py:263
  99.1 1.9 %shard_map.85 = bf16[48,32,128]{2,1,0:T(8,128)(2,1)S(1)} custom-call(s32[256]{0:T(256)S(1)} %compare_select_fusion.target_ref, bf16[256,32,128]{2,1,0:T(8,128)(2,1)S(1)} %bitcast.38), custom_call_target="tpu_custom_call" | custom-call | tf_op jit(solution)/shard_map/pallas_call | solution.py:348
  101.0 10.2 %shard_map.86 = bf16[4,12,32,128]{3,2,1,0:T(8,128)(2,1)S(1)} custom-call(bf16[4,12,32,128]{3,2,1,0:T(8,128)(2,1)S(1)} %bitcast.39), custom_call_target="tpu_custom_call" | custom-call | tf_op jit(solution)/shard_map/pallas_call | solution.py:263
  111.2 0.7 convert_reduce_fusion
  (12 shorter events, 0.7 us)
Async XLA Ops:
  3.0 96.0 %all-to-all-start = ((f32[8,1,32]{2,1,0:T(1,128)}), f32[8,1,32]{2,1,0:T(1,128)S(1)}, u32[]{:S(2)}, u32[]{:S(2)}) async-start(f32[8,1,32]{2,1,0:T(1,128)} %all_to_all.6), calls=%async_computation | async-start | bytes 8192 | tf_op jit(solution)/shard_map/all_to_all | solution.py:311
  14.5 50.8 %copy-start = (s32[128]{0:T(128)S(1)}, s32[128]{0:T(128)}, u32[]{:S(2)}) copy-start(s32[128]{0:T(128)} %row_ref.1) | copy-start | bytes 1540
